TPU v7x, 128 devices: a whole 4x4x4 slice. The times are simulated.
128 devices in a mesh: dp: 4 (over y_lo, core), code: 32 (over x, y_hi, z).
Axes of the slice: x: 4, y: 4 (y_hi: 2, y_lo: 2; y = y_hi * 2 + y_lo), z: 4, core: 2. Of those that a mesh axis runs over, the one named last changes fastest.
Arguments:
- latents: bfloat16 [2, 1024, 256], P(None, 'dp'), may hold values from -4 to 4
- cotangent: bfloat16 [2, 1024, 256], P(None, 'dp'), may hold values from -6 to 6
- saved_lse: float32 [2, 1024], P(None, 'dp'), as said below
- codebook: float32 [262144, 256], P(('dp', 'code')), may hold values from -4 to 4
- first_moment: float32 [262144, 256], P(('dp', 'code')), may hold values from -0.6 to 0.6
- second_moment: float32 [262144, 256], P(('dp', 'code')), may hold values from 0.001 to 0.1
Outputs:
- latent_grads: bfloat16 [2, 1024, 256], P(None, 'dp')
- new_codebook: float32 [262144, 256], P(('dp', 'code'))
- new_first: float32 [262144, 256], P(('dp', 'code'))
- new_second: float32 [262144, 256], P(('dp', 'code'))
Inputs may be any that keep to these rules, and one draw needn't show every extreme that they name: `saved_lse`: for each row, the log of the sum over all 262144 codes of exp of the logits of the weights step, from these latents and this codebook.
All inputs are finite; a program needn't handle non-finite values.
Results may differ from a plain program's by a relative error of at most 0.035.
Values may be sent and summed in bfloat16 or wider, within the bound.
A program may use at most 128 MiB of HBM per device.

v0:
```python
import jax
import jax.numpy as jnp
from jax import lax
from jax.sharding import PartitionSpec as P

ADAM_STEPS = 10


sharpness = 0.25
first_decay = 0.5
second_decay = 0.9
step_rate = 0.01
epsilon = 1e-08


def scores_of(rows_lat, rows_cot, saved, table):
    stacked = jnp.concatenate([rows_lat, rows_cot], axis=0)
    product = lax.dot_general(
        stacked, table, (((1,), (1,)), ((), ())), preferred_element_type=jnp.float32
    )
    row_total = rows_lat.shape[0]
    squares = jnp.sum(jnp.square(table.astype(jnp.float32)), axis=1)
    logits = sharpness * product[:row_total] - 0.5 * sharpness * squares[None, :]
    weights = jnp.exp(logits - saved[:, None])
    return (weights, product[row_total:])


def code_terms(weights, scaled, scaled_half, rows_lat, rows_cot, table):
    left = jnp.concatenate([weights.astype(jnp.bfloat16), scaled_half], axis=0)
    right = jnp.concatenate([rows_cot, rows_lat], axis=0)
    outer = lax.dot_general(
        left, right, (((0,), (0,)), ((), ())), preferred_element_type=jnp.float32
    )
    return outer - jnp.sum(scaled, axis=0)[:, None] * table.astype(jnp.float32)


def adam_update(grad, codebook, first_moment, second_moment):
    new_first = first_decay * first_moment + (1.0 - first_decay) * grad
    new_second = second_decay * second_moment + (1.0 - second_decay) * grad * grad
    first_hat = new_first / (1.0 - first_decay**ADAM_STEPS)
    second_hat = new_second / (1.0 - second_decay**ADAM_STEPS)
    new_codebook = codebook - step_rate * first_hat / (jnp.sqrt(second_hat) + epsilon)
    return (new_codebook, new_first, new_second)


def body(latents, cotangent, saved_lse, codebook, first_moment, second_moment):
    table = codebook.astype(jnp.bfloat16)
    own_rows = latents.shape[1]
    results = []
    rows_lat, rows_cot = (
        lax.all_gather(latents, "dp", axis=1, tiled=True),
        lax.all_gather(cotangent, "dp", axis=1, tiled=True),
    )
    rows_lse = lax.all_gather(saved_lse, "dp", axis=1, tiled=True)
    grad = jnp.zeros((table.shape[0], table.shape[1]), jnp.float32)
    for batch_index in range(latents.shape[0]):
        weights, inner_dots = scores_of(
            rows_lat[batch_index], rows_cot[batch_index], rows_lse[batch_index], table
        )
        row_ratio = lax.psum(jnp.sum(weights * inner_dots, axis=1), ("dp", "code"))
        scaled = sharpness * weights * (inner_dots - row_ratio[:, None])
        scaled_half = scaled.astype(jnp.bfloat16)
        whole = lax.psum(
            jnp.dot(scaled_half, table, preferred_element_type=jnp.float32), ("dp", "code")
        )
        mine = lax.dynamic_slice_in_dim(whole, lax.axis_index("dp") * own_rows, own_rows, 0)
        results.append(mine.astype(jnp.bfloat16))
        grad = grad + code_terms(
            weights, scaled, scaled_half, rows_lat[batch_index], rows_cot[batch_index], table
        )
    new_codebook, new_first, new_second = adam_update(grad, codebook, first_moment, second_moment)
    return (jnp.stack(results, axis=0), new_codebook, new_first, new_second)


def solution(mesh):
    placed = (
        P(None, "dp", None),
        P(None, "dp", None),
        P(None, "dp"),
        P(("dp", "code"), None),
        P(("dp", "code"), None),
        P(("dp", "code"), None),
    )
    return jax.shard_map(
        body,
        mesh=mesh,
        in_specs=placed,
        out_specs=(
            P(None, "dp", None),
            P(("dp", "code"), None),
            P(("dp", "code"), None),
            P(("dp", "code"), None),
        ),
        check_vma=False,
    )
```

profile of v0, /device:TPU:0, one launch (start us, length us, event | category | flops | bytes accessed | tf_op | source)
XLA Modules:
  0.0 323.8 jit_solution(10542318223992659285)
XLA Ops:
  7.2 0.0 all-gather.3.cloned.1.call-start
  7.2 0.7 all-gather.3.cloned.1.call-update
  7.9 0.0 all-gather.5.cloned.1.call-start
  7.9 0.7 all-gather.5.cloned.1.call-update
  8.7 5.3 %all_gather.11 = f32[2,1024]{1,0:T(2,128)S(1)} all-gather(f32[2,256]{1,0:T(2,128)} %param.8), channel_id=1, replica_groups=mesh['dp'=4,'code'=32] {'dp'}, dimensions={1}, use_global_device_ids=true | all-gather | bytes 10240 | tf_op jit(solution)/shard_map/all_gather | solution.py:54
  14.0 2.0 fusion.23
  15.9 16.9 %all-gather.3.cloned.1.call-done = bf16[2,1024,256]{2,1,0:T(8,128)(2,1)} async-done(((bf16[2,256,256]{2,1,0:T(8,128)(2,1)}), bf16[2,1024,256]{2,1,0:T(8,128)(2,1)}) %all-gather.3.cloned.1.call-update) | async-done | bytes 1048592 | tf_op jit(solution)/shard_map/all_gather | solution.py:51
  32.8 1.3 slice_bitcast_fusion.1
  34.1 0.0 copy-start.5
  34.1 0.0 copy-start.7
  34.1 22.0 %all-gather.5.cloned.1.call-done = bf16[2,1024,256]{2,1,0:T(8,128)(2,1)} async-done(((bf16[2,256,256]{2,1,0:T(8,128)(2,1)}), bf16[2,1024,256]{2,1,0:T(8,128)(2,1)}) %all-gather.5.cloned.1.call-update) | async-done | bytes 1048592 | tf_op jit(solution)/shard_map/all_gather | solution.py:52
  56.2 1.3 slice_bitcast_fusion
  57.4 0.0 copy-start.6
  57.5 0.0 copy-start.9
  57.5 2.4 fusion.25
  59.9 5.7 %copy-done.1 = f32[2048,2048]{1,0:T(8,128)} copy-done((f32[2048,2048]{1,0:T(8,128)}, f32[2048,2048]{1,0:T(8,128)S(1)}, u32[]{:S(2)}) %copy-start.1) | copy-done | bytes 16777240
  65.6 2.5 multiply_reduce_fusion.1
  68.1 66.5 %psum.28 = f32[1024]{0:T(1024)S(1)} all-reduce(f32[1024]{0:T(1024)S(1)} %multiply_reduce_fusion.1), channel_id=1, replica_groups=mesh['dp'=4,'code'=32] {'dp','code'}, use_global_device_ids=true, to_apply=%region_2.0 | all-reduce | flops 1024 | bytes 8192 | tf_op jit(solution)/shard_map/psum | solution.py:60
  134.6 0.0 copy-done.7
  134.6 2.4 fusion.29
  137.0 17.3 %fusion.39 = (f32[2048]{0:T(1024)S(1)}, f32[1024]{0:T(1024)S(1)}, bf16[1024,2048]{1,0:T(8,128)(2,1)}, bf16[1024,2048]{1,0:T(8,128)(2,1)}, bf16[1024,2048]{1,0:T(8,128)(2,1)}) fusion(f32[1024]{0:T(1024)S(1)} %psum.28, f32[2048,2048]{1,0:T(8,128)} %copy-done.1, f32[1024]{0:T(1024)S(1)} %bitcast.21, f32[2048]{0:T(1024)S(1)} %broadcast_multiply_fusion.1, ...), kind=kLoop, calls=%fused_computation.52 | loop fusion | flops 31454208 | bytes 46170112 | tf_op jit(solution)/shard_map/reduce_sum | solution.py:34
  154.3 62.6 %psum.30 = f32[1024]{0:T(1024)S(1)} all-reduce(f32[1024]{0:T(1024)S(1)} %get-tuple-element.5), channel_id=1, replica_groups=mesh['dp'=4,'code'=32] {'dp','code'}, use_global_device_ids=true, to_apply=%region_5.0 | all-reduce | flops 1024 | bytes 8192 | tf_op jit(solution)/shard_map/psum | solution.py:60
  216.9 7.6 %fusion.41 = (f32[2048]{0:T(1024)S(1)}, bf16[1024,2048]{1,0:T(8,128)(2,1)S(1)}) fusion(f32[1024]{0:T(1024)S(1)} %psum.30, f32[2048,2048]{1,0:T(8,128)} %copy-done, f32[1024]{0:T(1024)S(1)} %bitcast.23, f32[2048]{0:T(1024)S(1)} %broadcast_multiply_fusion.1), kind=kLoop, calls=%fused_computation.54 | loop fusion | flops 16775168 | bytes 20996096 | tf_op jit(solution)/shard_map/reduce_sum | solution.py:34
  224.5 2.2 fusion.54
  226.7 2.2 fusion.53
  229.0 0.4 copy-done.8
  229.3 0.2 copy-done.10
  229.6 4.2 %fusion.14 = f32[2048,256]{1,0:T(8,128)} fusion(bf16[1024,2048]{1,0:T(8,128)(2,1)S(1)} %get-tuple-element.13, bf16[1024,2048]{1,0:T(8,128)(2,1)S(1)} %copy-done.3, bf16[2048,256]{1,0:T(8,128)(2,1)S(1)} %get-tuple-element.11, bf16[1024,256]{1,0:T(8,128)(2,1)S(1)} %copy-done.8, bf16[1024,256]{1,0:T(8,128)(2,1)S(1)} %copy-done.10, f32[2048]{0:T(1024)S(1)} %get-tuple-element.12), kind=kOutput, calls=%fused_computation.24 | convolution fusion | flops 2167930880 | bytes 12591104 | tf_op jit(solution)/shard_map/dot_general | solution.py:31
  233.8 72.3 %all-reduce.2 = (bf16[1024,256]{1,0:T(8,128)(2,1)}, bf16[1024,256]{1,0:T(8,128)(2,1)}) all-reduce(f32[1024,256]{1,0:T(8,128)} %fusion.54, f32[1024,256]{1,0:T(8,128)} %fusion.53), channel_id=1, replica_groups=mesh['dp'=4,'code'=32] {'dp','code'}, use_global_device_ids=true, to_apply=%region_6.0 | all-reduce | flops 524288 | bytes 3145728 | tf_op jit(solution)/shard_map/psum | solution.py:63
  306.1 1.0 fusion.43
  307.1 0.7 pad_maximum_fusion
  307.8 9.2 %divide_subtract_fusion = (f32[2048,256]{1,0:T(8,128)}, f32[2048,256]{1,0:T(8,128)}, f32[2048,256]{1,0:T(8,128)}) fusion(f32[2048,256]{1,0:T(8,128)S(1)} %copy-done.4, f32[2048,256]{1,0:T(8,128)} %param.10, f32[2048,256]{1,0:T(8,128)} %param.11, f32[2048,256]{1,0:T(8,128)} %fusion.14, bf16[2048,256]{1,0:T(8,128)(2,1)S(1)} %get-tuple-element.11, ...), kind=kOutput, calls=%fused_computation.29 | convolution fusion | flops 2174222336 | bytes 25174016 | tf_op jit(solution)/shard_map/dot_general | solution.py:31
  (16 shorter events, 0.0 us)
Async XLA Ops:
  7.2 25.7 %all-gather.3.cloned.1.call-start = ((), (), s32[]{:S(2)}) async-start(), calls=%async_computation | async-start | bytes 1310720 | tf_op jit(solution)/shard_map/all_gather | solution.py:51
  7.9 48.3 %all-gather.5.cloned.1.call-start = ((), (), s32[]{:S(2)}) async-start(), calls=%async_computation.1 | async-start | bytes 1310720 | tf_op jit(solution)/shard_map/all_gather | solution.py:52
  34.1 25.7 %copy-start.5 = (bf16[1024,256]{1,0:T(8,128)(2,1)}, bf16[1024,256]{1,0:T(8,128)(2,1)S(1)}, u32[]{:S(2)}) copy-start(bf16[1024,256]{1,0:T(8,128)(2,1)S(1)} %get-tuple-element.19) | copy-start | bytes 1572868
  34.1 100.5 %copy-start.7 = (bf16[1024,256]{1,0:T(8,128)(2,1)}, bf16[1024,256]{1,0:T(8,128)(2,1)S(1)}, u32[]{:S(2)}) copy-start(bf16[1024,256]{1,0:T(8,128)(2,1)S(1)} %get-tuple-element.18) | copy-start | bytes 1572868
  57.4 2.4 copy-start.6
  57.5 77.2 %copy-start.9 = (bf16[1024,256]{1,0:T(8,128)(2,1)}, bf16[1024,256]{1,0:T(8,128)(2,1)S(1)}, u32[]{:S(2)}) copy-start(bf16[1024,256]{1,0:T(8,128)(2,1)S(1)} %get-tuple-element.20) | copy-start | bytes 1572868
  59.9 5.7 %copy-start.1 = (f32[2048,2048]{1,0:T(8,128)}, f32[2048,2048]{1,0:T(8,128)S(1)}, u32[]{:S(2)}) copy-start(f32[2048,2048]{1,0:T(8,128)S(1)} %fusion.25) | copy-start | bytes 50331652
  137.0 17.4 %copy-start = (f32[2048,2048]{1,0:T(8,128)}, f32[2048,2048]{1,0:T(8,128)S(1)}, u32[]{:S(2)}) copy-start(f32[2048,2048]{1,0:T(8,128)S(1)} %fusion.29) | copy-start | bytes 50331652
  224.5 2.3 copy-start.2
  226.7 2.3 copy-start.3
  226.7 2.6 copy-start.8
  226.7 2.8 copy-start.10
  229.6 78.3 %copy-start.4 = (f32[2048,256]{1,0:T(8,128)S(1)}, f32[2048,256]{1,0:T(8,128)}, u32[]{:S(2)}) copy-start(f32[2048,256]{1,0:T(8,128)} %param.9) | copy-start | bytes 6291460
Sparse Core Ops, SparseCore 0:
  9.7 23.1 all-gather.2
  34.5 21.6 all-gather.4
where the time goes:
time: 325 us; the launch traced here: 324 us
  blocking collectives  207 us (64%)
  waiting for transfers between devices  40.3 us (12%)
  other arithmetic  30.1 us (9%)
  matrix products  22.6 us (7%)
  between operations  14.2 us (4%)
  local copies, waits for them, and re-layouts  9.87 us (3%)
    psum x2, blocking collectives, body(): row_ratio = lax.psum(jnp.sum(weights * inner_dots, axis=1), ('dp', 'code'))  129 us
    psum x1, blocking collectives, body(): lax.psum(jnp.dot(scaled_half, table, preferred_element_type=jnp.float32),...  72.3 us
    reduce_sum x2, other arithmetic, code_terms(): return outer - jnp.sum(scaled, axis=0)[:, None] * table.astype(jnp.float32)  24.9 us
    all_gather x1, waiting for transfers between devices, body(): lax.all_gather(cotangent, 'dp', axis=1, tiled=True)  22 us
    all_gather x1, waiting for transfers between devices, body(): lax.all_gather(latents, 'dp', axis=1, tiled=True)  16.9 us
    dot_general x2, matrix products, code_terms(): lax.dot_general(left, right, (((0,), (0,)), ((), ())), preferred_element_...  13.4 us
  transfers between devices with their start and end apart: 2, of which 2 were waited for; matrix products, arithmetic and copies ran while one was open for 1% of the time, Pallas kernels for 0%

commit v1 on v0

v1 whole, which is shorter than its diff:
```python
import functools
import math

import jax
import jax.numpy as jnp
from jax import lax
from jax.experimental import pallas as pl
from jax.experimental.pallas import tpu as pltpu
from jax.sharding import PartitionSpec as P

MESH = pl.DeviceIdType.MESH
ADAM_STEPS = 10
sharpness = 0.25
first_decay = 0.5
second_decay = 0.9
step_rate = 0.01
epsilon = 1e-8

LOG2E = math.log2(math.e)
CODES = 2048
WIDTH = 256
ROWS = 256
BATCH = 1024
ALL = 2 * BATCH
F32, BF16 = jnp.float32, jnp.bfloat16


def place():
    dp, code = lax.axis_index("dp"), lax.axis_index("code")
    return code // 8, ((code // 4) % 2) * 2 + dp // 2, code % 4, dp % 2


def device(x, y, z, core):
    x, y, z, core = x % 4, y % 4, z % 4, core % 2
    return ((y % 2) * 2 + core, x * 8 + (y // 2) * 4 + z)


def dot_nt(a, b):
    return lax.dot_general(a, b, (((1,), (1,)), ((), ())), preferred_element_type=F32)


def dot(a, b):
    return jnp.dot(a, b, preferred_element_type=F32)


def aligned(v, n):
    return pl.multiple_of(v, n)


def kernel(
    lat_in, cot_in, lse_in, code_in, first_in, second_in,
    lg_out, code_out, first_out, second_out,
    lat, cot, lse, book, mom1, mom2, tab, tab_t, tab4, bias, weights, dots, scaled, grads, col_sum,
    part, part_y, part_s, part_xz, ratio,
    lg_part, lg_core, lg_pair, lg_y, lg_half, lg_xz, lg_final, lg_all,
    load_sem, gs_sem, gr_sem, fs_sem, fr_sem, cs_sem, cr_sem,
    ays_sem, ayr_sem, axs_sem, axr_sem,
    lcs_sem, lcr_sem, lys_sem, lyr_sem, lxs_sem, lxr_sem, lgs_sem, lgr_sem,
):
    x, y, z, core = place()
    y_lo, y_hi = y % 2, y // 2
    dp = y_lo * 2 + core
    part_no = x * 4 + z
    partner = device(x, y, z, core + 1)

    barrier = pltpu.get_barrier_semaphore()

    def yc_peer(i):
        return device(x, y + i // 2, z, core + i)

    def xz_peer(i):
        return device(x + i // 4, y, z + i, core)

    def code_peer(i):
        return device(x + i // 4, y + (i // 16) * 2, z + i, core)

    def signal_yc(i, _):
        pl.semaphore_signal(barrier, inc=1, device_id=yc_peer(i), device_id_type=MESH)
        return 0

    def signal_code(i, _):
        pl.semaphore_signal(barrier, inc=1, device_id=code_peer(i), device_id_type=MESH)
        return 0

    lax.fori_loop(1, 8, signal_yc, 0)
    lax.fori_loop(1, 32, signal_code, 0)

    book_copy = pltpu.make_async_copy(code_in, book, load_sem.at[0])
    book_copy.start()
    mom1_copy = pltpu.make_async_copy(first_in, mom1, load_sem.at[1])
    mom2_copy = pltpu.make_async_copy(second_in, mom2, load_sem.at[2])

    def rows_of(mb, owner):
        return pl.ds(aligned(mb * BATCH + owner * ROWS, ROWS), ROWS)

    own_copies = []
    for mb in range(2):
        own_copies += [
            pltpu.make_async_copy(lat_in.at[mb], lat.at[rows_of(mb, dp)], load_sem.at[3 + mb]),
            pltpu.make_async_copy(cot_in.at[mb], cot.at[rows_of(mb, dp)], load_sem.at[5 + mb]),
        ]
    own_copies.append(pltpu.make_async_copy(lse_in, lse.at[dp], load_sem.at[7]))
    for c in own_copies:
        c.start()
    mom1_copy.start()
    mom2_copy.start()

    book_copy.wait()

    def make_table(i, _):
        at = pl.ds(aligned(i * 256, 256), 256)
        t = book[at, :].astype(BF16)
        tab[at, :] = t
        tab_t[:, at] = t.T
        wide = t.astype(F32)
        tab4[at, :] = (wide * sharpness).astype(BF16)
        squares = jnp.sum(wide * wide, axis=1, keepdims=True) * (0.5 * sharpness * LOG2E)
        bias[at, :] = jnp.broadcast_to(squares, (256, 128))
        col_sum[at, :] = jnp.zeros((256, 128), F32)
        return 0

    lax.fori_loop(0, CODES // 256, make_table, 0)

    for c in own_copies:
        c.wait()

    def pass_one(mb, owner):
        at = rows_of(mb, owner)
        rows_lat, rows_cot = lat[at, :], cot[at, :]
        shift = lse[owner, 0:1, mb * ROWS : (mb + 1) * ROWS] * LOG2E
        step = 256
        total = jnp.zeros((8, ROWS), F32)
        for k in range(0, CODES, step):
            t = tab4[k : k + step, :]
            b = bias[k : k + step, :]
            logits = dot_nt(t, rows_lat)
            inner = dot_nt(t, rows_cot)
            w = jnp.exp2(logits * LOG2E - jnp.concatenate([b, b], axis=1) - shift)
            total = total + jnp.sum((w * inner).reshape(step // 8, 8, ROWS), axis=0)
            weights[k : k + step, at] = w.astype(BF16)
            dots[k : k + step, at] = inner
        row = jnp.sum(total, axis=0, keepdims=True)
        part[mb, pl.ds(owner * 2, 1), :] = row[:, :128]
        part[mb, pl.ds(owner * 2 + 1, 1), :] = row[:, 128:]


    pass_one(0, dp)
    pass_one(1, dp)

    pl.semaphore_wait(barrier, 38)

    def remote(src, dst, send, recv, to):
        return pltpu.make_async_remote_copy(
            src_ref=src, dst_ref=dst, send_sem=send, recv_sem=recv, device_id=to, device_id_type=MESH
        )

    def row_copies(owner, sends, recvs, to):
        copies = [remote(lse.at[owner], lse.at[owner], sends.at[4], recvs.at[4], to)]
        for mb in range(2):
            at = rows_of(mb, owner)
            copies.append(remote(lat.at[at], lat.at[at], sends.at[2 * mb], recvs.at[2 * mb], to))
            copies.append(remote(cot.at[at], cot.at[at], sends.at[2 * mb + 1], recvs.at[2 * mb + 1], to))
        return copies

    to_partner = row_copies(dp, cs_sem, cr_sem, partner)
    to_y = row_copies(dp, gs_sem, gr_sem, device(x, y + 1 - 2 * core, z, core))
    for c in to_y + to_partner:
        c.start()

    other = (1 - y_lo) * 2 + core
    forward = row_copies(other, fs_sem, fr_sem, partner)
    mate = y_lo * 2 + 1 - core
    other_mate = (1 - y_lo) * 2 + 1 - core

    for i in range(3):
        to_partner[i].wait_recv()
    pass_one(0, mate)
    for i in range(3):
        to_y[i].wait_recv()
        forward[i].start()
    for i in range(3, 5):
        to_partner[i].wait_recv()
    pass_one(1, mate)
    pass_one(0, other)
    for i in range(3, 5):
        to_y[i].wait_recv()
        forward[i].start()
    for i in range(3):
        forward[i].wait_recv()
    pass_one(0, other_mate)

    def ratio_y(mb):
        return [
            remote(part.at[mb], part_y.at[mb, i], ays_sem.at[mb, i], ayr_sem.at[mb, i], yc_peer(i))
            for i in range(1, 8)
        ]

    def ratio_xz(mb):
        return [
            remote(part_s.at[mb], part_xz.at[mb, i], axs_sem.at[mb, i], axr_sem.at[mb, i], xz_peer(i))
            for i in range(1, 16)
        ]

    ry, rx = [ratio_y(0), ratio_y(1)], [ratio_xz(0), ratio_xz(1)]

    def ratio_first(mb):
        for c in ry[mb]:
            c.start()

    def ratio_second(mb):
        for c in ry[mb]:
            c.wait()
        part_s[mb] = part[mb] + jnp.sum(part_y[mb, 1:8], axis=0)
        for c in rx[mb]:
            c.start()

    def ratio_end(mb):
        for c in rx[mb]:
            c.wait()
        ratio[mb] = part_s[mb] + jnp.sum(part_xz[mb, 1:16], axis=0)

    ratio_first(0)
    pass_one(1, other)
    for i in range(3, 5):
        forward[i].wait_recv()
    ratio_second(0)
    pass_one(1, other_mate)
    ratio_first(1)

    def grads_weights(i, _):
        at = pl.ds(aligned(i * 256, 256), 256)
        grads[at, :] = dot(weights[at, :], cot[...])
        return 0

    lax.fori_loop(0, 4, grads_weights, 0)
    ratio_second(1)
    lax.fori_loop(4, 8, grads_weights, 0)

    def scale(mb, u):
        at = pl.ds(aligned(mb * BATCH + u * ROWS, ROWS), ROWS)
        r = jnp.concatenate([ratio[mb, pl.ds(u * 2, 1), :], ratio[mb, pl.ds(u * 2 + 1, 1), :]], axis=1)
        step = 256
        for k in range(0, CODES, step):
            s = weights[k : k + step, at].astype(F32) * (dots[k : k + step, at] - r)
            scaled[k : k + step, at] = s.astype(BF16)
            col_sum[k : k + step, :] += s[:, :128] + s[:, 128:]

    def latent(mb, u):
        at = pl.ds(aligned(mb * BATCH + u * ROWS, ROWS), ROWS)
        lg_part[mb, u] = dot(tab_t[...], scaled[:, at]).astype(BF16)

    def second_pass(mb):
        scale(mb, 0)

        def step(u, _):
            scale(mb, u)
            latent(mb, u - 1)
            return 0

        lax.fori_loop(1, 4, step, 0)
        latent(mb, 3)

    l_core = [
        [
            remote(lg_part.at[mb, h * 2 + 1 - core], lg_core.at[mb, h], lcs_sem.at[mb, h], lcr_sem.at[mb, h], partner)
            for h in range(2)
        ]
        for mb in range(2)
    ]

    def l_y_copy(mb, i):
        to_y_no = (y + i) % 4
        src = lg_pair.at[mb, to_y_no % 2, pl.ds(aligned((to_y_no // 2) * 128, 128), 128)]
        return remote(src, lg_y.at[mb, i], lys_sem.at[mb, i], lyr_sem.at[mb, i], device(x, y + i, z, core))

    l_y = [[l_y_copy(mb, i) for i in range(1, 4)] for mb in range(2)]

    def piece(no):
        return pl.ds(aligned((no // 2) * 16, 16), 16), pl.ds(aligned((no % 2) * 128, 128), 128)

    def l_xz_copy(mb, i):
        to_no = ((x + i // 4) % 4) * 4 + (z + i) % 4
        r, c = piece(to_no)
        return remote(lg_half.at[mb, r, c], lg_xz.at[mb, i], lxs_sem.at[mb, i], lxr_sem.at[mb, i], xz_peer(i))

    def final_place(mb):
        r, c = piece(part_no)
        return lg_all.at[mb, pl.ds(aligned(y_hi * 128 + (part_no // 2) * 16, 16), 16), c]

    def l_all_copy(mb, i):
        return remote(lg_final.at[mb], final_place(mb), lgs_sem.at[mb, i], lgr_sem.at[mb, i], code_peer(i))

    l_xz = [[l_xz_copy(mb, i) for i in range(1, 16)] for mb in range(2)]
    l_all = [[l_all_copy(mb, i) for i in range(1, 32)] for mb in range(2)]

    def latent_0(mb):
        for c in l_core[mb]:
            c.start()

    def latent_1(mb):
        for c in l_core[mb]:
            c.wait()
        for h in range(2):
            lg_pair[mb, h] = (lg_part[mb, h * 2 + core].astype(F32) + lg_core[mb, h].astype(F32)).astype(BF16)
        for c in l_y[mb]:
            c.start()

    def latent_2(mb):
        for c in l_y[mb]:
            c.wait()
        total = lg_pair[mb, y_lo, pl.ds(aligned(y_hi * 128, 128), 128), :].astype(F32)
        for i in range(1, 4):
            total = total + lg_y[mb, i].astype(F32)
        lg_half[mb] = total.astype(BF16)
        for c in l_xz[mb]:
            c.start()

    def latent_3(mb):
        for c in l_xz[mb]:
            c.wait()
        r, c = piece(part_no)
        total = lg_half[mb, r, c].astype(F32)
        for i in range(1, 16):
            total = total + lg_xz[mb, i].astype(F32)
        lg_final[mb] = total.astype(BF16)
        final_place(mb)[...] = total.astype(BF16)
        for c in l_all[mb]:
            c.start()

    def latent_4(mb):
        for c in l_all[mb]:
            c.wait()
        lg_out[mb] = lg_all[mb].T

    def adam(i, _):
        at = pl.ds(aligned(i * 256, 256), 256)
        t = tab[at, :].astype(F32)
        sums = jnp.sum(col_sum[at, :], axis=1, keepdims=True)
        grad = grads[at, :] + dot(scaled[at, :], lat[...]) - sums * t
        new_first = first_decay * mom1[at, :] + (1.0 - first_decay) * grad
        new_second = second_decay * mom2[at, :] + (1.0 - second_decay) * grad * grad
        first_hat = new_first * (1.0 / (1.0 - first_decay**ADAM_STEPS))
        second_hat = new_second * (1.0 / (1.0 - second_decay**ADAM_STEPS))
        code_out[at, :] = book[at, :] - step_rate * first_hat / (jnp.sqrt(second_hat) + epsilon)
        first_out[at, :] = new_first
        second_out[at, :] = new_second
        return 0

    ratio_end(0)
    second_pass(0)
    latent_0(0)
    ratio_end(1)
    second_pass(1)
    latent_0(1)
    latent_1(0)
    mom1_copy.wait()
    mom2_copy.wait()
    lax.fori_loop(0, 1, adam, 0)
    latent_1(1)
    lax.fori_loop(1, 2, adam, 0)
    latent_2(0)
    lax.fori_loop(2, 4, adam, 0)
    latent_2(1)
    lax.fori_loop(4, 5, adam, 0)
    latent_3(0)
    lax.fori_loop(5, 8, adam, 0)
    latent_3(1)
    latent_4(0)
    latent_4(1)
    for c in to_y + to_partner + forward:
        c.wait_send()


def body(latents, cotangent, saved_lse, codebook, first_moment, second_moment):
    lse_rows = jnp.broadcast_to(saved_lse.reshape(1, 2 * ROWS), (8, 2 * ROWS))
    dma = pltpu.SemaphoreType.DMA
    any_spec, vmem_spec = pl.BlockSpec(memory_space=pl.ANY), pl.BlockSpec(memory_space=pltpu.VMEM)
    code_array = jax.ShapeDtypeStruct((CODES, WIDTH), F32)
    lg, new_code, new_first, new_second = pl.pallas_call(
        kernel,
        name="soft_codebook",
        out_shape=(jax.ShapeDtypeStruct((2, ROWS, WIDTH), BF16), code_array, code_array, code_array),
        in_specs=[any_spec] * 6,
        out_specs=[vmem_spec] * 4,
        scratch_shapes=[
            pltpu.VMEM((ALL, WIDTH), BF16),
            pltpu.VMEM((ALL, WIDTH), BF16),
            pltpu.VMEM((4, 8, 2 * ROWS), F32),
            pltpu.VMEM((CODES, WIDTH), F32),
            pltpu.VMEM((CODES, WIDTH), F32),
            pltpu.VMEM((CODES, WIDTH), F32),
            pltpu.VMEM((CODES, WIDTH), BF16),
            pltpu.VMEM((WIDTH, CODES), BF16),
            pltpu.VMEM((CODES, WIDTH), BF16),
            pltpu.VMEM((CODES, 128), F32),
            pltpu.VMEM((CODES, ALL), BF16),
            pltpu.VMEM((CODES, ALL), F32),
            pltpu.VMEM((CODES, ALL), BF16),
            pltpu.VMEM((CODES, WIDTH), F32),
            pltpu.VMEM((CODES, 128), F32),
            pltpu.VMEM((2, 8, 128), F32),
            pltpu.VMEM((2, 8, 8, 128), F32),
            pltpu.VMEM((2, 8, 128), F32),
            pltpu.VMEM((2, 16, 8, 128), F32),
            pltpu.VMEM((2, 8, 128), F32),
            pltpu.VMEM((2, 4, WIDTH, ROWS), BF16),
            pltpu.VMEM((2, 2, WIDTH, ROWS), BF16),
            pltpu.VMEM((2, 2, WIDTH, ROWS), BF16),
            pltpu.VMEM((2, 4, WIDTH // 2, ROWS), BF16),
            pltpu.VMEM((2, WIDTH // 2, ROWS), BF16),
            pltpu.VMEM((2, 16, 16, 128), BF16),
            pltpu.VMEM((2, 16, 128), BF16),
            pltpu.VMEM((2, WIDTH, ROWS), BF16),
            dma((8,)),
            dma((5,)), dma((5,)), dma((5,)), dma((5,)), dma((5,)), dma((5,)),
            dma((2, 8)), dma((2, 8)), dma((2, 16)), dma((2, 16)),
            dma((2, 2)), dma((2, 2)), dma((2, 4)), dma((2, 4)), dma((2, 16)), dma((2, 16)), dma((2, 32)), dma((2, 32)),
        ],
        compiler_params=pltpu.CompilerParams(
            collective_id=0, has_side_effects=True, vmem_limit_bytes=60 * 1024 * 1024
        ),
    )(latents, cotangent, lse_rows, codebook, first_moment, second_moment)
    return lg, new_code, new_first, new_second


def solution(mesh):
    rows, codes = P(None, "dp", None), P(("dp", "code"), None)
    return jax.shard_map(
        body,
        mesh=mesh,
        in_specs=(rows, rows, P(None, "dp"), codes, codes, codes),
        out_specs=(rows, codes, codes, codes),
        check_vma=False,
    )
```

time: 325 us -> 74.5 us (0.23)
  blocking collectives: 207 us -> 0 us
  Pallas kernels: 0 us -> 63.9 us
  waiting for transfers between devices: 40.3 us -> 0 us
  other arithmetic: 30.1 us -> 0 us
  matrix products: 22.6 us -> 0 us
  between operations: 14.2 us -> 0.64 us
    psum x3 -> x0, blocking collectives: 201 us -> none  [the longest x2 129 us: body(): row_ratio = lax.psum(jnp.sum(weights * inner_dots, axis=1), ('dp', 'code'))]
    pallas_call x0 -> x1, Pallas kernels: none -> 63.9 us  [body(): pl.pallas_call(kernel, name='soft_codebook', out_shape=(jax.ShapeDtypeStr...]
    all_gather x2 -> x0, waiting for transfers between devices: 38.9 us -> none  [the longest x1 22 us: body(): lax.all_gather(cotangent, 'dp', axis=1, tiled=True)]
    reduce_sum x4 -> x0, other arithmetic: 29.4 us -> none  [the longest x2 24.9 us: code_terms(): return outer - jnp.sum(scaled, axis=0)[:, None] * table.astype(jnp.float32)]
    dot_general x6 -> x0, matrix products: 22.6 us -> none  [the longest x2 13.4 us: code_terms(): lax.dot_general(left, right, (((0,), (0,)), ((), ())), preferred_element_...]
    all_gather x1 -> x0, blocking collectives: 5.3 us -> none  [body(): rows_lse = lax.all_gather(saved_lse, 'dp', axis=1, tiled=True)]
    unnamed x22 -> x9, local copies, waits for them, and re-layouts: 6.35 us -> 9.22 us
  transfers between devices with their start and end apart: 2 -> 0, of which waited for: 2 -> 0; matrix products, arithmetic and copies ran while one was open for 1% -> 0% of each run, Pallas kernels for 0% -> 0%
where the time goes in v1:
time: 74.5 us; the launch traced here: 74.3 us
  Pallas kernels  63.9 us (86%)
  local copies, waits for them, and re-layouts  9.83 us (13%)
    pallas_call x1, Pallas kernels, body(): pl.pallas_call(kernel, name='soft_codebook', out_shape=(jax.ShapeDtypeStr...  63.9 us
    unnamed x9, local copies, waits for them, and re-layouts  9.22 us

profile of v1, /device:TPU:0, one launch (start us, length us, event | category | flops | bytes accessed | tf_op | source)
XLA Modules:
  0.0 74.3 jit_solution(7143705686823265097)
XLA Ops:
  0.6 0.7 copy.10
  1.3 0.6 broadcast_in_dim.8.lse_in
  1.9 63.9 %soft_codebook.1 = (bf16[2,256,256]{2,1,0:T(8,128)(2,1)}, f32[2048,256]{1,0:T(8,128)}, f32[2048,256]{1,0:T(8,128)}, f32[2048,256]{1,0:T(8,128)}) custom-call(bf16[2,256,256]{2,1,0:T(8,128)(2,1)} %lat_in.1, bf16[2,256,256]{2,1,0:T(8,128)(2,1)} %cot_in.1, f32[8,512]{1,0:T(8,128)} %broadcast_in_dim.8.lse_in, f32[2048,256]{1,0:T(8,128)} %code_in.1, ...), custom_call_target="tpu_custom_call" | custom-call | tf_op jit(solution)/shard_map/soft_codebook/pallas_call | solution.py:379
  65.8 1.7 %copy.15 = bf16[2,256,256]{2,1,0:T(8,128)(2,1)} copy(bf16[2,256,256]{2,1,0:T(8,128)(2,1)} %get-tuple-element.8) | data formatting | bytes 524288
  67.5 0.0 copy-start.1
  67.5 3.2 %copy.16 = f32[2048,256]{1,0:T(8,128)} copy(f32[2048,256]{1,0:T(8,128)} %get-tuple-element.9) | data formatting | bytes 4194304
  70.7 0.0 copy-done.1
  70.7 0.0 copy-start
  70.7 1.3 %copy.17 = f32[2048,256]{1,0:T(8,128)} copy(f32[2048,256]{1,0:T(8,128)S(1)} %copy-done.1) | data formatting | bytes 4194304
  72.0 1.0 %copy-done = f32[2048,256]{1,0:T(8,128)S(1)} copy-done((f32[2048,256]{1,0:T(8,128)S(1)}, f32[2048,256]{1,0:T(8,128)}, u32[]{:S(2)}) %copy-start) | copy-done | bytes 2097176
  73.0 1.3 %copy.18 = f32[2048,256]{1,0:T(8,128)} copy(f32[2048,256]{1,0:T(8,128)S(1)} %copy-done) | data formatting | bytes 4194304
Async XLA Ops:
  67.5 3.2 %copy-start.1 = (f32[2048,256]{1,0:T(8,128)S(1)}, f32[2048,256]{1,0:T(8,128)}, u32[]{:S(2)}) copy-start(f32[2048,256]{1,0:T(8,128)} %get-tuple-element.10) | copy-start | bytes 6291460
  70.7 2.3 %copy-start = (f32[2048,256]{1,0:T(8,128)S(1)}, f32[2048,256]{1,0:T(8,128)}, u32[]{:S(2)}) copy-start(f32[2048,256]{1,0:T(8,128)} %get-tuple-element.11) | copy-start | bytes 6291460

commit v2 on v1

v2 whole, which is shorter than its diff:
```python
import functools
import math

import jax
import jax.numpy as jnp
from jax import lax
from jax.experimental import pallas as pl
from jax.experimental.pallas import tpu as pltpu
from jax.sharding import PartitionSpec as P

MESH = pl.DeviceIdType.MESH
ADAM_STEPS = 10
sharpness = 0.25
first_decay = 0.5
second_decay = 0.9
step_rate = 0.01
epsilon = 1e-8

LOG2E = math.log2(math.e)
CODES = 2048
WIDTH = 256
ROWS = 256
BATCH = 1024
ALL = 2 * BATCH
F32, BF16 = jnp.float32, jnp.bfloat16


def place():
    dp, code = lax.axis_index("dp"), lax.axis_index("code")
    return code // 8, ((code // 4) % 2) * 2 + dp // 2, code % 4, dp % 2


def device(x, y, z, core):
    x, y, z, core = x % 4, y % 4, z % 4, core % 2
    return ((y % 2) * 2 + core, x * 8 + (y // 2) * 4 + z)


def dot_nt(a, b):
    return lax.dot_general(a, b, (((1,), (1,)), ((), ())), preferred_element_type=F32)


def dot(a, b):
    return jnp.dot(a, b, preferred_element_type=F32)


def aligned(v, n):
    return pl.multiple_of(v, n)


def kernel(
    lat_in, cot_in, lse_in, code_in, first_in, second_in,
    lg_out, code_out, first_out, second_out,
    lat, cot, lse, tab, tab_t, bias, weights, dots, grads, col_sum,
    part, part_y, part_s, part_xz, ratio,
    lg_part, lg_core, lg_pair, lg_y, lg_half, lg_xz, lg_final, lg_all, hop_sem,
    load_sem, gs_sem, gr_sem, fs_sem, fr_sem, cs_sem, cr_sem,
    ays_sem, ayr_sem, axs_sem, axr_sem,
    lcs_sem, lcr_sem, lys_sem, lyr_sem, lxs_sem, lxr_sem, lgs_sem, lgr_sem,
):
    x, y, z, core = place()
    y_lo, y_hi = y % 2, y // 2
    dp = y_lo * 2 + core
    part_no = x * 4 + z
    partner = device(x, y, z, core + 1)

    barrier = pltpu.get_barrier_semaphore()
    along = {
        "core": [partner],
        "x": [device(x + 1, y, z, core), device(x + 3, y, z, core)],
        "y": [device(x, y + 1, z, core), device(x, y + 3, z, core)],
        "z": [device(x, y, z + 1, core), device(x, y, z + 3, core)],
    }
    for peers in along.values():
        for to in peers:
            pl.semaphore_signal(barrier, inc=1, device_id=to, device_id_type=MESH)

    def hear_send(no, axis):
        for to in along[axis]:
            pl.semaphore_signal(hop_sem.at[no], inc=1, device_id=to, device_id_type=MESH)

    def hear_wait(no, axis):
        pl.semaphore_wait(hop_sem.at[no], len(along[axis]))

    def yc_peer(i):
        return device(x, y + i // 2, z, core + i)

    def xz_peer(i):
        return device(x + i // 4, y, z + i, core)

    def code_peer(i):
        return device(x + i // 4, y + (i // 16) * 2, z + i, core)

    book_copy = pltpu.make_async_copy(code_in, code_out, load_sem.at[0])
    mom1_copy = pltpu.make_async_copy(first_in, first_out, load_sem.at[1])
    mom2_copy = pltpu.make_async_copy(second_in, second_out, load_sem.at[2])

    def rows_of(mb, owner):
        return pl.ds(aligned(mb * BATCH + owner * ROWS, ROWS), ROWS)

    own_copies = []
    for mb in range(2):
        own_copies += [
            pltpu.make_async_copy(lat_in.at[mb], lat.at[rows_of(mb, dp)], load_sem.at[3 + mb]),
            pltpu.make_async_copy(cot_in.at[mb], cot.at[rows_of(mb, dp)], load_sem.at[5 + mb]),
        ]
    own_copies.append(pltpu.make_async_copy(lse_in, lse.at[dp], load_sem.at[7]))
    for c in own_copies:
        c.start()
    book_copy.start()
    mom1_copy.start()
    mom2_copy.start()

    def remote(src, dst, send, recv, to):
        return pltpu.make_async_remote_copy(
            src_ref=src, dst_ref=dst, send_sem=send, recv_sem=recv, device_id=to, device_id_type=MESH
        )

    def row_copies(owner, sends, recvs, to):
        copies = [remote(lse.at[owner], lse.at[owner], sends.at[4], recvs.at[4], to)]
        for mb in range(2):
            at = rows_of(mb, owner)
            copies.append(remote(lat.at[at], lat.at[at], sends.at[2 * mb], recvs.at[2 * mb], to))
            copies.append(remote(cot.at[at], cot.at[at], sends.at[2 * mb + 1], recvs.at[2 * mb + 1], to))
        return copies

    to_partner = row_copies(dp, cs_sem, cr_sem, partner)
    to_y = row_copies(dp, gs_sem, gr_sem, device(x, y + 1 - 2 * core, z, core))
    pl.semaphore_wait(barrier, 7)
    for c in own_copies:
        c.wait()
    for c in to_y + to_partner:
        c.start()
    hear_send(0, "y")

    book_copy.wait()

    def make_table(i, _):
        at = pl.ds(aligned(i * 256, 256), 256)
        t = code_out[at, :].astype(BF16)
        tab[at, :] = t
        tab_t[:, at] = t.T
        wide = t.astype(F32)
        squares = jnp.sum(wide * wide, axis=1, keepdims=True) * (0.5 * sharpness * LOG2E)
        bias[at, :] = jnp.broadcast_to(squares, (256, 128))
        return 0

    lax.fori_loop(0, CODES // 256, make_table, 0)

    def pass_one(pairs):
        places = [rows_of(mb, owner) for mb, owner in pairs]
        shifts = [lse[owner, mb : mb + 1, :] * LOG2E for mb, owner in pairs]
        totals = [jnp.zeros((8, ROWS), F32) for _ in pairs]
        step = 256
        for k in range(0, CODES, step):
            t = tab[k : k + step, :]
            b = bias[k : k + step, :]
            b = jnp.concatenate([b, b], axis=1)
            for i, at in enumerate(places):
                logits = dot_nt(t, lat[at, :])
                inner = dot_nt(t, cot[at, :])
                w = jnp.exp2(logits * (sharpness * LOG2E) - b - shifts[i])
                totals[i] = totals[i] + jnp.sum((w * inner).reshape(step // 8, 8, ROWS), axis=0)
                weights[k : k + step, at] = w.astype(BF16)
                dots[k : k + step, at] = inner
        for (mb, owner), total in zip(pairs, totals):
            row = jnp.sum(total, axis=0, keepdims=True)
            part[mb, pl.ds(owner * 2, 1), :] = row[:, :128]
            part[mb, pl.ds(owner * 2 + 1, 1), :] = row[:, 128:]

    def grads_weights(mb, half, first):
        at = pl.ds(aligned(mb * BATCH + half * 512, 512), 512)
        product = dot(weights[:, at], cot[at, :])
        if first:
            grads[...] = product
        else:
            grads[...] += product

    other = (1 - y_lo) * 2 + core
    forward = row_copies(other, fs_sem, fr_sem, partner)
    mate = y_lo * 2 + 1 - core
    other_mate = (1 - y_lo) * 2 + 1 - core

    def ratio_y(mb):
        return [
            remote(part.at[mb], part_y.at[mb, i], ays_sem.at[mb, i], ayr_sem.at[mb, i], yc_peer(i))
            for i in range(1, 8)
        ]

    def ratio_xz(mb):
        return [
            remote(part_s.at[mb], part_xz.at[mb, i], axs_sem.at[mb, i], axr_sem.at[mb, i], xz_peer(i))
            for i in range(1, 16)
        ]

    ry, rx = [ratio_y(0), ratio_y(1)], [ratio_xz(0), ratio_xz(1)]

    def ratio_first(mb):
        for c in ry[mb]:
            c.start()

    def ratio_second(mb):
        for c in ry[mb]:
            c.wait()
        part_s[mb] = part[mb] + jnp.sum(part_y[mb, 1:8], axis=0)
        for c in rx[mb]:
            c.start()

    def ratio_end(mb):
        for c in rx[mb]:
            c.wait()
        ratio[mb] = part_s[mb] + jnp.sum(part_xz[mb, 1:16], axis=0)

    pass_one([(0, dp), (1, dp)])
    hear_wait(0, "y")
    hear_send(1, "core")
    for c in to_partner:
        c.wait_recv()
    pass_one([(0, mate), (1, mate)])
    hear_wait(1, "core")
    hear_send(2, "x")
    for c in to_y[:3]:
        c.wait_recv()
    for c in forward[:3]:
        c.start()
    grads_weights(0, y_lo, True)
    hear_wait(2, "x")
    hear_send(3, "x")
    for c in forward[:3]:
        c.wait_recv()
    pass_one([(0, other), (0, other_mate)])
    ratio_first(0)
    hear_wait(3, "x")
    hear_send(4, "z")
    for c in to_y[3:]:
        c.wait_recv()
    for c in forward[3:]:
        c.start()
    pass_one([(1, other)])
    hear_wait(4, "z")
    hear_send(5, "z")
    for c in forward[3:]:
        c.wait_recv()
    pass_one([(1, other_mate)])
    ratio_first(1)
    hear_wait(5, "z")
    ratio_second(0)
    grads_weights(1, y_lo, False)
    ratio_second(1)
    grads_weights(0, 1 - y_lo, False)
    grads_weights(1, 1 - y_lo, False)

    def scale(mb):
        r = [
            jnp.concatenate([ratio[mb, 2 * u : 2 * u + 1, :], ratio[mb, 2 * u + 1 : 2 * u + 2, :]], axis=1)
            for u in range(4)
        ]
        step = 256
        for k in range(0, CODES, step):
            sums = None
            for u in range(4):
                at = slice(mb * BATCH + u * ROWS, mb * BATCH + (u + 1) * ROWS)
                s = weights[k : k + step, at].astype(F32) * (dots[k : k + step, at] - r[u])
                weights[k : k + step, at] = s.astype(BF16)
                half = s[:, :128] + s[:, 128:]
                sums = half if sums is None else sums + half
            if mb == 0:
                col_sum[k : k + step, :] = sums
            else:
                col_sum[k : k + step, :] += sums

    def latent(mb):
        whole = dot(tab_t[...], weights[:, mb * BATCH : (mb + 1) * BATCH]) * sharpness
        for u in range(4):
            lg_part[mb, u] = whole[:, u * ROWS : (u + 1) * ROWS].astype(BF16)

    def grads_scaled(mb):
        at = slice(mb * BATCH, (mb + 1) * BATCH)
        grads[...] += dot(weights[:, at], lat[at, :]) * sharpness

    l_core = [
        [
            remote(lg_part.at[mb, h * 2 + 1 - core], lg_core.at[mb, h], lcs_sem.at[mb, h], lcr_sem.at[mb, h], partner)
            for h in range(2)
        ]
        for mb in range(2)
    ]

    def l_y_copy(mb, i):
        to_y_no = (y + i) % 4
        src = lg_pair.at[mb, to_y_no % 2, pl.ds(aligned((to_y_no // 2) * 128, 128), 128)]
        return remote(src, lg_y.at[mb, i], lys_sem.at[mb, i], lyr_sem.at[mb, i], device(x, y + i, z, core))

    l_y = [[l_y_copy(mb, i) for i in range(1, 4)] for mb in range(2)]

    def piece(no):
        return pl.ds(aligned((no // 2) * 16, 16), 16), pl.ds(aligned((no % 2) * 128, 128), 128)

    def l_xz_copy(mb, i):
        to_no = ((x + i // 4) % 4) * 4 + (z + i) % 4
        r, c = piece(to_no)
        return remote(lg_half.at[mb, r, c], lg_xz.at[mb, i], lxs_sem.at[mb, i], lxr_sem.at[mb, i], xz_peer(i))

    def final_place(mb):
        r, c = piece(part_no)
        return lg_all.at[mb, pl.ds(aligned(y_hi * 128 + (part_no // 2) * 16, 16), 16), c]

    def l_all_copy(mb, i):
        return remote(lg_final.at[mb], final_place(mb), lgs_sem.at[mb, i], lgr_sem.at[mb, i], code_peer(i))

    l_xz = [[l_xz_copy(mb, i) for i in range(1, 16)] for mb in range(2)]
    l_all = [[l_all_copy(mb, i) for i in range(1, 32)] for mb in range(2)]

    def latent_0(mb):
        for c in l_core[mb]:
            c.start()

    def latent_1(mb):
        for c in l_core[mb]:
            c.wait()
        for h in range(2):
            lg_pair[mb, h] = (lg_part[mb, h * 2 + core].astype(F32) + lg_core[mb, h].astype(F32)).astype(BF16)
        for c in l_y[mb]:
            c.start()

    def latent_2(mb):
        for c in l_y[mb]:
            c.wait()
        total = lg_pair[mb, y_lo, pl.ds(aligned(y_hi * 128, 128), 128), :].astype(F32)
        for i in range(1, 4):
            total = total + lg_y[mb, i].astype(F32)
        lg_half[mb] = total.astype(BF16)
        for c in l_xz[mb]:
            c.start()

    def latent_3(mb):
        for c in l_xz[mb]:
            c.wait()
        r, c = piece(part_no)
        total = lg_half[mb, r, c].astype(F32)
        for i in range(1, 16):
            total = total + lg_xz[mb, i].astype(F32)
        lg_final[mb] = total.astype(BF16)
        final_place(mb)[...] = total.astype(BF16)
        for c in l_all[mb]:
            c.start()

    def latent_4(mb):
        for c in l_all[mb]:
            c.wait()
        lg_out[mb] = lg_all[mb]

    def adam(i, _):
        at = pl.ds(aligned(i * 256, 256), 256)
        t = tab[at, :].astype(F32)
        sums = jnp.sum(col_sum[at, :], axis=1, keepdims=True) * sharpness
        grad = grads[at, :] - sums * t
        new_first = first_decay * first_out[at, :] + (1.0 - first_decay) * grad
        new_second = second_decay * second_out[at, :] + (1.0 - second_decay) * grad * grad
        first_hat = new_first * (1.0 / (1.0 - first_decay**ADAM_STEPS))
        second_hat = new_second * (1.0 / (1.0 - second_decay**ADAM_STEPS))
        code_out[at, :] = code_out[at, :] - step_rate * first_hat / (jnp.sqrt(second_hat) + epsilon)
        first_out[at, :] = new_first
        second_out[at, :] = new_second
        return 0

    ratio_end(0)
    scale(0)
    latent(0)
    latent_0(0)
    ratio_end(1)
    scale(1)
    latent_1(0)
    latent(1)
    latent_0(1)
    grads_scaled(0)
    latent_1(1)
    latent_2(0)
    grads_scaled(1)
    mom1_copy.wait()
    mom2_copy.wait()
    lax.fori_loop(0, 2, adam, 0)
    latent_2(1)
    lax.fori_loop(2, 5, adam, 0)
    latent_3(0)
    lax.fori_loop(5, 8, adam, 0)
    latent_3(1)
    latent_4(0)
    latent_4(1)
    for c in to_y + to_partner + forward:
        c.wait_send()


def write_out(lg_in, code_in, first_in, second_in, lg_out, code_out, first_out, second_out, sems):
    copies = [
        pltpu.make_async_copy(src, dst, sems.at[i])
        for i, (src, dst) in enumerate([(code_in, code_out), (first_in, first_out), (second_in, second_out)])
    ]
    for c in copies:
        c.start()
    for mb in range(2):
        lg_out[mb] = lg_in[mb].T
    for c in copies:
        c.wait()


def body(*arrays):
    dma = pltpu.SemaphoreType.DMA
    any_spec, vmem_spec = pl.BlockSpec(memory_space=pl.ANY), pl.BlockSpec(memory_space=pltpu.VMEM)
    code_shape, rows_shape = (CODES, WIDTH), (2, ROWS, WIDTH)
    parts = pl.pallas_call(
        kernel,
        name="soft_codebook",
        out_shape=(pltpu.VMEM((2, WIDTH, ROWS), BF16),) + (pltpu.VMEM(code_shape, F32),) * 3,
        in_specs=[pl.BlockSpec(memory_space=pltpu.HBM)] * 6,
        out_specs=[vmem_spec] * 4,
        scratch_shapes=[
            pltpu.VMEM((ALL, WIDTH), BF16),
            pltpu.VMEM((ALL, WIDTH), BF16),
            pltpu.VMEM((4, 2, ROWS), F32),
            pltpu.VMEM((CODES, WIDTH), BF16),
            pltpu.VMEM((WIDTH, CODES), BF16),
            pltpu.VMEM((CODES, 128), F32),
            pltpu.VMEM((CODES, ALL), BF16),
            pltpu.VMEM((CODES, ALL), F32),
            pltpu.VMEM((CODES, WIDTH), F32),
            pltpu.VMEM((CODES, 128), F32),
            pltpu.VMEM((2, 8, 128), F32),
            pltpu.VMEM((2, 8, 8, 128), F32),
            pltpu.VMEM((2, 8, 128), F32),
            pltpu.VMEM((2, 16, 8, 128), F32),
            pltpu.VMEM((2, 8, 128), F32),
            pltpu.VMEM((2, 4, WIDTH, ROWS), BF16),
            pltpu.VMEM((2, 2, WIDTH, ROWS), BF16),
            pltpu.VMEM((2, 2, WIDTH, ROWS), BF16),
            pltpu.VMEM((2, 4, WIDTH // 2, ROWS), BF16),
            pltpu.VMEM((2, WIDTH // 2, ROWS), BF16),
            pltpu.VMEM((2, 16, 16, 128), BF16),
            pltpu.VMEM((2, 16, 128), BF16),
            pltpu.VMEM((2, WIDTH, ROWS), BF16),
            pltpu.SemaphoreType.REGULAR((6,)),
            dma((8,)),
            dma((5,)), dma((5,)), dma((5,)), dma((5,)), dma((5,)), dma((5,)),
            dma((2, 8)), dma((2, 8)), dma((2, 16)), dma((2, 16)),
            dma((2, 2)), dma((2, 2)), dma((2, 4)), dma((2, 4)), dma((2, 16)), dma((2, 16)), dma((2, 32)), dma((2, 32)),
        ],
        compiler_params=pltpu.CompilerParams(
            collective_id=0, has_side_effects=True, vmem_limit_bytes=40 * 1024 * 1024
        ),
    )(*[pltpu.with_memory_space_constraint(a, pltpu.HBM) for a in arrays])
    code_array = jax.ShapeDtypeStruct(code_shape, F32)
    return pl.pallas_call(
        write_out,
        name="write_out",
        out_shape=(jax.ShapeDtypeStruct(rows_shape, BF16), code_array, code_array, code_array),
        in_specs=[vmem_spec] * 4,
        out_specs=[vmem_spec] + [any_spec] * 3,
        scratch_shapes=[dma((3,))],
        compiler_params=pltpu.CompilerParams(vmem_limit_bytes=8 * 1024 * 1024),
    )(*[pltpu.with_memory_space_constraint(p, pltpu.VMEM) for p in parts])


def solution(mesh):
    rows, codes = P(None, "dp", None), P(("dp", "code"), None)
    return jax.shard_map(
        body,
        mesh=mesh,
        in_specs=(rows, rows, P(None, "dp"), codes, codes, codes),
        out_specs=(rows, codes, codes, codes),
        check_vma=False,
    )
```

time: 74.5 us -> 57.6 us (0.77)
  local copies, waits for them, and re-layouts: 9.83 us -> 0 us
  Pallas kernels: 63.9 us -> 56.7 us
    unnamed x9 -> x0, local copies, waits for them, and re-layouts: 9.22 us -> none
    pallas_call x1 -> x2, Pallas kernels: 63.9 us -> 56.7 us  [the longest x1 53.3 us: body(): pl.pallas_call(kernel, name='soft_codebook', out_shape=(pltpu.VMEM((2, WI...]
where the time goes in v2:
time: 57.6 us; the launch traced here: 57.5 us
  Pallas kernels  56.7 us (98%)
  between operations  0.8 us (1%)
    pallas_call x1, Pallas kernels, body(): pl.pallas_call(kernel, name='soft_codebook', out_shape=(pltpu.VMEM((2, WI...  53.3 us
    pallas_call x1, Pallas kernels, body(): pl.pallas_call(write_out, name='write_out', out_shape=(jax.ShapeDtypeStru...  3.45 us

profile of v2, /device:TPU:0, one launch (start us, length us, event | category | flops | bytes accessed | tf_op | source)
XLA Modules:
  0.0 57.5 jit_solution(5629170085088968355)
XLA Ops:
  0.6 53.3 %soft_codebook.1 = (bf16[2,256,256]{2,1,0:T(8,128)(2,1)S(1)}, f32[2048,256]{1,0:T(8,128)S(1)}, f32[2048,256]{1,0:T(8,128)S(1)}, f32[2048,256]{1,0:T(8,128)S(1)}) custom-call(bf16[2,256,256]{2,1,0:T(8,128)(2,1)} %lat_in.1, bf16[2,256,256]{2,1,0:T(8,128)(2,1)} %cot_in.1, f32[2,256]{1,0:T(2,128)} %lse_in.1, f32[2048,256]{1,0:T(8,128)} %code_in.1, ...), custom_call_target="tpu_custom_call" | custom-call | tf_op jit(solution)/shard_map/soft_codebook/pallas_call | solution.py:410
  53.9 3.5 %write_out.1 = (bf16[2,256,256]{2,1,0:T(8,128)(2,1)}, f32[2048,256]{1,0:T(8,128)}, f32[2048,256]{1,0:T(8,128)}, f32[2048,256]{1,0:T(8,128)}) custom-call(bf16[2,256,256]{2,1,0:T(8,128)(2,1)S(1)} %get-tuple-element.8.lg_in, f32[2048,256]{1,0:T(8,128)S(1)} %get-tuple-element.9.code_in, f32[2048,256]{1,0:T(8,128)S(1)} %get-tuple-element.10.first_in, ...), custom_call_target="tpu_custom_call" | custom-call | tf_op jit(solution)/shard_map/write_out/pallas_call | solution.py:451

commit v3 on v2

--- a/solution.py
+++ b/solution.py
@@ -50,12 +50,12 @@
 def kernel(
     lat_in, cot_in, lse_in, code_in, first_in, second_in,
     lg_out, code_out, first_out, second_out,
-    lat, cot, lse, tab, tab_t, bias, weights, dots, grads, col_sum,
+    lat, lat_scaled, cot, lse, tab, tab_t, bias, weights, dots, grads, col_sum,
     part, part_y, part_s, part_xz, ratio,
-    lg_part, lg_core, lg_pair, lg_y, lg_half, lg_xz, lg_final, lg_all, hop_sem,
+    lg_part, lg_core, lg_pair, lg_sum, lg_final, lg_all, hop_sem,
     load_sem, gs_sem, gr_sem, fs_sem, fr_sem, cs_sem, cr_sem,
     ays_sem, ayr_sem, axs_sem, axr_sem,
-    lcs_sem, lcr_sem, lys_sem, lyr_sem, lxs_sem, lxr_sem, lgs_sem, lgr_sem,
+    lcs_sem, lcr_sem, lxs_sem, lxr_sem, lgs_sem, lgr_sem,
 ):
     x, y, z, core = place()
     y_lo, y_hi = y % 2, y // 2
@@ -104,32 +104,44 @@
             pltpu.make_async_copy(cot_in.at[mb], cot.at[rows_of(mb, dp)], load_sem.at[5 + mb]),
         ]
     own_copies.append(pltpu.make_async_copy(lse_in, lse.at[dp], load_sem.at[7]))
+    book_copy.start()
     for c in own_copies:
         c.start()
-    book_copy.start()
-    mom1_copy.start()
-    mom2_copy.start()
 
     def remote(src, dst, send, recv, to):
         return pltpu.make_async_remote_copy(
             src_ref=src, dst_ref=dst, send_sem=send, recv_sem=recv, device_id=to, device_id_type=MESH
         )
 
+    def wait_bytes(ref, sem):
+        pltpu.make_async_copy(ref, ref, sem).wait()
+
     def row_copies(owner, sends, recvs, to):
-        copies = [remote(lse.at[owner], lse.at[owner], sends.at[4], recvs.at[4], to)]
+        copies = [[], []]
         for mb in range(2):
             at = rows_of(mb, owner)
-            copies.append(remote(lat.at[at], lat.at[at], sends.at[2 * mb], recvs.at[2 * mb], to))
-            copies.append(remote(cot.at[at], cot.at[at], sends.at[2 * mb + 1], recvs.at[2 * mb + 1], to))
+            for ref in (lat, cot):
+                copies[mb].append(remote(ref.at[at], ref.at[at], sends.at[mb], recvs.at[mb], to))
+        copies[0].append(remote(lse.at[owner], lse.at[owner], sends.at[2], recvs.at[2], to))
         return copies
+
+    def start_rows(copies, mb):
+        for c in copies[mb]:
+            c.start()
+
+    def wait_rows(sems, mb):
+        wait_bytes(lat.at[pl.ds(0, 2 * ROWS)], sems.at[mb])
+        if mb == 0:
+            wait_bytes(lse.at[0], sems.at[2])
 
     to_partner = row_copies(dp, cs_sem, cr_sem, partner)
     to_y = row_copies(dp, gs_sem, gr_sem, device(x, y + 1 - 2 * core, z, core))
     pl.semaphore_wait(barrier, 7)
     for c in own_copies:
         c.wait()
-    for c in to_y + to_partner:
-        c.start()
+    for mb in range(2):
+        start_rows(to_y, mb)
+        start_rows(to_partner, mb)
     hear_send(0, "y")
 
     book_copy.wait()
@@ -138,13 +150,15 @@
         at = pl.ds(aligned(i * 256, 256), 256)
         t = code_out[at, :].astype(BF16)
         tab[at, :] = t
-        tab_t[:, at] = t.T
         wide = t.astype(F32)
+        tab_t[:, at] = (wide * sharpness).astype(BF16).T
         squares = jnp.sum(wide * wide, axis=1, keepdims=True) * (0.5 * sharpness * LOG2E)
         bias[at, :] = jnp.broadcast_to(squares, (256, 128))
         return 0
 
     lax.fori_loop(0, CODES // 256, make_table, 0)
+    mom1_copy.start()
+    mom2_copy.start()
 
     def pass_one(pairs):
         places = [rows_of(mb, owner) for mb, owner in pairs]
@@ -182,13 +196,13 @@
 
     def ratio_y(mb):
         return [
-            remote(part.at[mb], part_y.at[mb, i], ays_sem.at[mb, i], ayr_sem.at[mb, i], yc_peer(i))
+            remote(part.at[mb], part_y.at[mb, i], ays_sem.at[mb], ayr_sem.at[mb], yc_peer(i))
             for i in range(1, 8)
         ]
 
     def ratio_xz(mb):
         return [
-            remote(part_s.at[mb], part_xz.at[mb, i], axs_sem.at[mb, i], axr_sem.at[mb, i], xz_peer(i))
+            remote(part_s.at[mb], part_xz.at[mb, i], axs_sem.at[mb], axr_sem.at[mb], xz_peer(i))
             for i in range(1, 16)
         ]
 
@@ -199,115 +213,120 @@
             c.start()
 
     def ratio_second(mb):
-        for c in ry[mb]:
-            c.wait()
+        for sem in (ays_sem, ayr_sem):
+            wait_bytes(part_y.at[mb, pl.ds(1, 7)], sem.at[mb])
         part_s[mb] = part[mb] + jnp.sum(part_y[mb, 1:8], axis=0)
         for c in rx[mb]:
             c.start()
 
     def ratio_end(mb):
-        for c in rx[mb]:
-            c.wait()
+        for sem in (axs_sem, axr_sem):
+            wait_bytes(part_xz.at[mb, pl.ds(1, 15)], sem.at[mb])
         ratio[mb] = part_s[mb] + jnp.sum(part_xz[mb, 1:16], axis=0)
 
     pass_one([(0, dp), (1, dp)])
     hear_wait(0, "y")
     hear_send(1, "core")
-    for c in to_partner:
-        c.wait_recv()
+    wait_rows(cr_sem, 0)
+    wait_rows(cr_sem, 1)
     pass_one([(0, mate), (1, mate)])
     hear_wait(1, "core")
     hear_send(2, "x")
-    for c in to_y[:3]:
-        c.wait_recv()
-    for c in forward[:3]:
-        c.start()
     grads_weights(0, y_lo, True)
     hear_wait(2, "x")
     hear_send(3, "x")
-    for c in forward[:3]:
-        c.wait_recv()
-    pass_one([(0, other), (0, other_mate)])
-    ratio_first(0)
+    wait_rows(gr_sem, 0)
+    start_rows(forward, 0)
+    pass_one([(0, other)])
     hear_wait(3, "x")
     hear_send(4, "z")
-    for c in to_y[3:]:
-        c.wait_recv()
-    for c in forward[3:]:
-        c.start()
-    pass_one([(1, other)])
+    wait_rows(fr_sem, 0)
+    pass_one([(0, other_mate)])
+    ratio_first(0)
     hear_wait(4, "z")
     hear_send(5, "z")
-    for c in forward[3:]:
-        c.wait_recv()
+    wait_rows(gr_sem, 1)
+    start_rows(forward, 1)
+    pass_one([(1, other)])
+    hear_wait(5, "z")
+    wait_rows(fr_sem, 1)
     pass_one([(1, other_mate)])
     ratio_first(1)
-    hear_wait(5, "z")
     ratio_second(0)
     grads_weights(1, y_lo, False)
     ratio_second(1)
     grads_weights(0, 1 - y_lo, False)
     grads_weights(1, 1 - y_lo, False)
-
-    def scale(mb):
+    lat_scaled[...] = (lat[...].astype(F32) * sharpness).astype(BF16)
+
+    def scale(mb, half):
         r = [
             jnp.concatenate([ratio[mb, 2 * u : 2 * u + 1, :], ratio[mb, 2 * u + 1 : 2 * u + 2, :]], axis=1)
-            for u in range(4)
+            for u in (2 * half, 2 * half + 1)
         ]
         step = 256
         for k in range(0, CODES, step):
             sums = None
-            for u in range(4):
-                at = slice(mb * BATCH + u * ROWS, mb * BATCH + (u + 1) * ROWS)
+            for u in range(2):
+                start = mb * BATCH + (2 * half + u) * ROWS
+                at = slice(start, start + ROWS)
                 s = weights[k : k + step, at].astype(F32) * (dots[k : k + step, at] - r[u])
                 weights[k : k + step, at] = s.astype(BF16)
-                half = s[:, :128] + s[:, 128:]
-                sums = half if sums is None else sums + half
-            if mb == 0:
+                pair = s[:, :128] + s[:, 128:]
+                sums = pair if sums is None else sums + pair
+            if mb == 0 and half == 0:
                 col_sum[k : k + step, :] = sums
             else:
                 col_sum[k : k + step, :] += sums
 
-    def latent(mb):
-        whole = dot(tab_t[...], weights[:, mb * BATCH : (mb + 1) * BATCH]) * sharpness
-        for u in range(4):
-            lg_part[mb, u] = whole[:, u * ROWS : (u + 1) * ROWS].astype(BF16)
-
-    def grads_scaled(mb):
-        at = slice(mb * BATCH, (mb + 1) * BATCH)
-        grads[...] += dot(weights[:, at], lat[at, :]) * sharpness
+    def latent(mb, half):
+        start = mb * BATCH + half * 512
+        product = dot(tab_t[...], weights[:, start : start + 512])
+        for u in range(2):
+            lg_part[mb, 2 * half + u] = product[:, u * ROWS : (u + 1) * ROWS].astype(BF16)
+
+    def second_pass(mb):
+        scale(mb, 0)
+        latent(mb, 0)
+        scale(mb, 1)
+        latent(mb, 1)
+
+    def grads_scaled(mb, half):
+        start = mb * BATCH + half * 512
+        at = slice(start, start + 512)
+        grads[...] += dot(weights[:, at], lat_scaled[at, :])
 
     l_core = [
         [
-            remote(lg_part.at[mb, h * 2 + 1 - core], lg_core.at[mb, h], lcs_sem.at[mb, h], lcr_sem.at[mb, h], partner)
+            remote(lg_part.at[mb, h * 2 + 1 - core], lg_core.at[mb, h], lcs_sem.at[mb], lcr_sem.at[mb], partner)
             for h in range(2)
         ]
         for mb in range(2)
     ]
 
-    def l_y_copy(mb, i):
-        to_y_no = (y + i) % 4
-        src = lg_pair.at[mb, to_y_no % 2, pl.ds(aligned((to_y_no // 2) * 128, 128), 128)]
-        return remote(src, lg_y.at[mb, i], lys_sem.at[mb, i], lyr_sem.at[mb, i], device(x, y + i, z, core))
-
-    l_y = [[l_y_copy(mb, i) for i in range(1, 4)] for mb in range(2)]
-
-    def piece(no):
-        return pl.ds(aligned((no // 2) * 16, 16), 16), pl.ds(aligned((no % 2) * 128, 128), 128)
-
-    def l_xz_copy(mb, i):
-        to_no = ((x + i // 4) % 4) * 4 + (z + i) % 4
-        r, c = piece(to_no)
-        return remote(lg_half.at[mb, r, c], lg_xz.at[mb, i], lxs_sem.at[mb, i], lxr_sem.at[mb, i], xz_peer(i))
+    def place_of(no, hi):
+        return (
+            pl.ds(aligned(hi * 128 + (no // 2) * 16, 16), 16),
+            pl.ds(aligned((no % 2) * 128, 128), 128),
+        )
+
+    def chip_peer(i):
+        return device(x + i // 16, y + (i // 4) % 4, z + i, core)
+
+    def l_sum_copy(mb, i):
+        to_y_no = (y + (i // 4) % 4) % 4
+        rows, cols = place_of(((x + i // 16) % 4) * 4 + (z + i) % 4, to_y_no // 2)
+        src = lg_pair.at[mb, to_y_no % 2, rows, cols]
+        return remote(src, lg_sum.at[mb, i], lxs_sem.at[mb], lxr_sem.at[mb], chip_peer(i))
 
     def final_place(mb):
-        r, c = piece(part_no)
-        return lg_all.at[mb, pl.ds(aligned(y_hi * 128 + (part_no // 2) * 16, 16), 16), c]
+        rows, cols = place_of(part_no, y_hi)
+        return lg_all.at[mb, rows, cols]
 
     def l_all_copy(mb, i):
-        return remote(lg_final.at[mb], final_place(mb), lgs_sem.at[mb, i], lgr_sem.at[mb, i], code_peer(i))
-
-    l_xz = [[l_xz_copy(mb, i) for i in range(1, 16)] for mb in range(2)]
+        return remote(lg_final.at[mb], final_place(mb), lgs_sem.at[mb], lgr_sem.at[mb], code_peer(i))
+
+    l_sum = [[l_sum_copy(mb, i) for i in range(1, 64)] for mb in range(2)]
     l_all = [[l_all_copy(mb, i) for i in range(1, 32)] for mb in range(2)]
 
     def latent_0(mb):
@@ -315,38 +334,27 @@
             c.start()
 
     def latent_1(mb):
-        for c in l_core[mb]:
-            c.wait()
+        for sem in (lcs_sem, lcr_sem):
+            wait_bytes(lg_core.at[mb], sem.at[mb])
         for h in range(2):
             lg_pair[mb, h] = (lg_part[mb, h * 2 + core].astype(F32) + lg_core[mb, h].astype(F32)).astype(BF16)
-        for c in l_y[mb]:
+        rows, cols = place_of(part_no, y_hi)
+        lg_sum[mb, 0] = lg_pair[mb, y_lo, rows, cols]
+        for c in l_sum[mb]:
             c.start()
 
     def latent_2(mb):
-        for c in l_y[mb]:
-            c.wait()
-        total = lg_pair[mb, y_lo, pl.ds(aligned(y_hi * 128, 128), 128), :].astype(F32)
-        for i in range(1, 4):
-            total = total + lg_y[mb, i].astype(F32)
-        lg_half[mb] = total.astype(BF16)
-        for c in l_xz[mb]:
+        for sem in (lxs_sem, lxr_sem):
+            wait_bytes(lg_sum.at[mb, pl.ds(1, 63)], sem.at[mb])
+        total = jnp.sum(lg_sum[mb].astype(F32), axis=0).astype(BF16)
+        lg_final[mb] = total
+        final_place(mb)[...] = total
+        for c in l_all[mb]:
             c.start()
 
     def latent_3(mb):
-        for c in l_xz[mb]:
-            c.wait()
-        r, c = piece(part_no)
-        total = lg_half[mb, r, c].astype(F32)
-        for i in range(1, 16):
-            total = total + lg_xz[mb, i].astype(F32)
-        lg_final[mb] = total.astype(BF16)
-        final_place(mb)[...] = total.astype(BF16)
-        for c in l_all[mb]:
-            c.start()
-
-    def latent_4(mb):
-        for c in l_all[mb]:
-            c.wait()
+        for sem in (lgs_sem, lgr_sem):
+            wait_bytes(lg_sum.at[mb, pl.ds(1, 31)], sem.at[mb])
         lg_out[mb] = lg_all[mb]
 
     def adam(i, _):
@@ -364,30 +372,30 @@
         return 0
 
     ratio_end(0)
-    scale(0)
-    latent(0)
+    second_pass(0)
     latent_0(0)
     ratio_end(1)
-    scale(1)
+    scale(1, 0)
     latent_1(0)
-    latent(1)
+    latent(1, 0)
+    scale(1, 1)
+    latent(1, 1)
     latent_0(1)
-    grads_scaled(0)
+    grads_scaled(0, 0)
     latent_1(1)
-    latent_2(0)
-    grads_scaled(1)
+    grads_scaled(0, 1)
+    grads_scaled(1, 0)
+    grads_scaled(1, 1)
     mom1_copy.wait()
     mom2_copy.wait()
-    lax.fori_loop(0, 2, adam, 0)
+    latent_2(0)
+    lax.fori_loop(0, 8, adam, 0)
     latent_2(1)
-    lax.fori_loop(2, 5, adam, 0)
     latent_3(0)
-    lax.fori_loop(5, 8, adam, 0)
     latent_3(1)
-    latent_4(0)
-    latent_4(1)
-    for c in to_y + to_partner + forward:
-        c.wait_send()
+    for sems in (cs_sem, gs_sem, fs_sem):
+        wait_rows(sems, 0)
+        wait_rows(sems, 1)
 
 
 def write_out(lg_in, code_in, first_in, second_in, lg_out, code_out, first_out, second_out, sems):
@@ -414,6 +422,7 @@
         in_specs=[pl.BlockSpec(memory_space=pltpu.HBM)] * 6,
         out_specs=[vmem_spec] * 4,
         scratch_shapes=[
+            pltpu.VMEM((ALL, WIDTH), BF16),
             pltpu.VMEM((ALL, WIDTH), BF16),
             pltpu.VMEM((ALL, WIDTH), BF16),
             pltpu.VMEM((4, 2, ROWS), F32),
@@ -432,16 +441,14 @@
             pltpu.VMEM((2, 4, WIDTH, ROWS), BF16),
             pltpu.VMEM((2, 2, WIDTH, ROWS), BF16),
             pltpu.VMEM((2, 2, WIDTH, ROWS), BF16),
-            pltpu.VMEM((2, 4, WIDTH // 2, ROWS), BF16),
-            pltpu.VMEM((2, WIDTH // 2, ROWS), BF16),
-            pltpu.VMEM((2, 16, 16, 128), BF16),
+            pltpu.VMEM((2, 64, 16, 128), BF16),
             pltpu.VMEM((2, 16, 128), BF16),
             pltpu.VMEM((2, WIDTH, ROWS), BF16),
             pltpu.SemaphoreType.REGULAR((6,)),
             dma((8,)),
-            dma((5,)), dma((5,)), dma((5,)), dma((5,)), dma((5,)), dma((5,)),
-            dma((2, 8)), dma((2, 8)), dma((2, 16)), dma((2, 16)),
-            dma((2, 2)), dma((2, 2)), dma((2, 4)), dma((2, 4)), dma((2, 16)), dma((2, 16)), dma((2, 32)), dma((2, 32)),
+            dma((3,)), dma((3,)), dma((3,)), dma((3,)), dma((3,)), dma((3,)),
+            dma((2,)), dma((2,)), dma((2,)), dma((2,)),
+            dma((2,)), dma((2,)), dma((2,)), dma((2,)), dma((2,)), dma((2,)),
         ],
         compiler_params=pltpu.CompilerParams(
             collective_id=0, has_side_effects=True, vmem_limit_bytes=40 * 1024 * 1024

time: 57.6 us -> 51.2 us (0.89)
  Pallas kernels: 56.7 us -> 50.3 us
    pallas_call x1, Pallas kernels: 53.3 us -> 46.9 us  [body(): pl.pallas_call(kernel, name='soft_codebook', out_shape=(pltpu.VMEM((2, WI...]
where the time goes in v3:
time: 51.2 us; the launch traced here: 51.1 us
  Pallas kernels  50.3 us (98%)
  between operations  0.8 us (2%)
    pallas_call x1, Pallas kernels, body(): pl.pallas_call(kernel, name='soft_codebook', out_shape=(pltpu.VMEM((2, WI...  46.9 us
    pallas_call x1, Pallas kernels, body(): pl.pallas_call(write_out, name='write_out', out_shape=(jax.ShapeDtypeStru...  3.45 us

profile of v3, /device:TPU:0, one launch (start us, length us, event | category | flops | bytes accessed | tf_op | source)
XLA Modules:
  0.0 51.1 jit_solution(12329224235172519763)
XLA Ops:
  0.6 46.9 %soft_codebook.1 = (bf16[2,256,256]{2,1,0:T(8,128)(2,1)S(1)}, f32[2048,256]{1,0:T(8,128)S(1)}, f32[2048,256]{1,0:T(8,128)S(1)}, f32[2048,256]{1,0:T(8,128)S(1)}) custom-call(bf16[2,256,256]{2,1,0:T(8,128)(2,1)} %lat_in.1, bf16[2,256,256]{2,1,0:T(8,128)(2,1)} %cot_in.1, f32[2,256]{1,0:T(2,128)} %lse_in.1, f32[2048,256]{1,0:T(8,128)} %code_in.1, ...), custom_call_target="tpu_custom_call" | custom-call | tf_op jit(solution)/shard_map/soft_codebook/pallas_call | solution.py:418
  47.5 3.5 %write_out.1 = (bf16[2,256,256]{2,1,0:T(8,128)(2,1)}, f32[2048,256]{1,0:T(8,128)}, f32[2048,256]{1,0:T(8,128)}, f32[2048,256]{1,0:T(8,128)}) custom-call(bf16[2,256,256]{2,1,0:T(8,128)(2,1)S(1)} %get-tuple-element.8.lg_in, f32[2048,256]{1,0:T(8,128)S(1)} %get-tuple-element.9.code_in, f32[2048,256]{1,0:T(8,128)S(1)} %get-tuple-element.10.first_in, ...), custom_call_target="tpu_custom_call" | custom-call | tf_op jit(solution)/shard_map/write_out/pallas_call | solution.py:458

commit v4 on v3

--- a/solution.py
+++ b/solution.py
@@ -50,7 +50,7 @@
 def kernel(
     lat_in, cot_in, lse_in, code_in, first_in, second_in,
     lg_out, code_out, first_out, second_out,
-    lat, lat_scaled, cot, lse, tab, tab_t, bias, weights, dots, grads, col_sum,
+    lat, cot, lse, tab, tab_t, bias, weights, scaled, dots, grads, col_sum,
     part, part_y, part_s, part_xz, ratio,
     lg_part, lg_core, lg_pair, lg_sum, lg_final, lg_all, hop_sem,
     load_sem, gs_sem, gr_sem, fs_sem, fr_sem, cs_sem, cr_sem,
@@ -104,9 +104,9 @@
             pltpu.make_async_copy(cot_in.at[mb], cot.at[rows_of(mb, dp)], load_sem.at[5 + mb]),
         ]
     own_copies.append(pltpu.make_async_copy(lse_in, lse.at[dp], load_sem.at[7]))
-    book_copy.start()
     for c in own_copies:
         c.start()
+    book_copy.start()
 
     def remote(src, dst, send, recv, to):
         return pltpu.make_async_remote_copy(
@@ -116,13 +116,13 @@
     def wait_bytes(ref, sem):
         pltpu.make_async_copy(ref, ref, sem).wait()
 
-    def row_copies(owner, sends, recvs, to):
+    def row_copies(owner, sends, recvs, to_lat, to_cot):
         copies = [[], []]
         for mb in range(2):
             at = rows_of(mb, owner)
-            for ref in (lat, cot):
+            for ref, to in ((lat, to_lat), (cot, to_cot)):
                 copies[mb].append(remote(ref.at[at], ref.at[at], sends.at[mb], recvs.at[mb], to))
-        copies[0].append(remote(lse.at[owner], lse.at[owner], sends.at[2], recvs.at[2], to))
+        copies[0].append(remote(lse.at[owner], lse.at[owner], sends.at[2], recvs.at[2], to_lat))
         return copies
 
     def start_rows(copies, mb):
@@ -134,31 +134,36 @@
         if mb == 0:
             wait_bytes(lse.at[0], sems.at[2])
 
-    to_partner = row_copies(dp, cs_sem, cr_sem, partner)
-    to_y = row_copies(dp, gs_sem, gr_sem, device(x, y + 1 - 2 * core, z, core))
+    to_partner = row_copies(dp, cs_sem, cr_sem, partner, partner)
+    to_y = row_copies(dp, gs_sem, gr_sem, device(x, y + 1, z, core), device(x, y + 3, z, core))
     pl.semaphore_wait(barrier, 7)
     for c in own_copies:
         c.wait()
-    for mb in range(2):
-        start_rows(to_y, mb)
-        start_rows(to_partner, mb)
+    start_rows(to_y, 0)
     hear_send(0, "y")
+    start_rows(to_partner, 0)
+    start_rows(to_partner, 1)
 
     book_copy.wait()
+    hear_wait(0, "y")
+    hear_send(1, "core")
 
     def make_table(i, _):
         at = pl.ds(aligned(i * 256, 256), 256)
         t = code_out[at, :].astype(BF16)
         tab[at, :] = t
         wide = t.astype(F32)
-        tab_t[:, at] = (wide * sharpness).astype(BF16).T
+        tab_t[:, at] = t.T
         squares = jnp.sum(wide * wide, axis=1, keepdims=True) * (0.5 * sharpness * LOG2E)
         bias[at, :] = jnp.broadcast_to(squares, (256, 128))
         return 0
 
     lax.fori_loop(0, CODES // 256, make_table, 0)
+    start_rows(to_y, 1)
     mom1_copy.start()
     mom2_copy.start()
+    hear_wait(1, "core")
+    hear_send(2, "x")
 
     def pass_one(pairs):
         places = [rows_of(mb, owner) for mb, owner in pairs]
@@ -171,7 +176,7 @@
             b = jnp.concatenate([b, b], axis=1)
             for i, at in enumerate(places):
                 logits = dot_nt(t, lat[at, :])
-                inner = dot_nt(t, cot[at, :])
+                inner = dot_nt(t, cot[at, :]) * sharpness
                 w = jnp.exp2(logits * (sharpness * LOG2E) - b - shifts[i])
                 totals[i] = totals[i] + jnp.sum((w * inner).reshape(step // 8, 8, ROWS), axis=0)
                 weights[k : k + step, at] = w.astype(BF16)
@@ -190,7 +195,7 @@
             grads[...] += product
 
     other = (1 - y_lo) * 2 + core
-    forward = row_copies(other, fs_sem, fr_sem, partner)
+    forward = row_copies(other, fs_sem, fr_sem, partner, partner)
     mate = y_lo * 2 + 1 - core
     other_mate = (1 - y_lo) * 2 + 1 - core
 
@@ -225,26 +230,21 @@
         ratio[mb] = part_s[mb] + jnp.sum(part_xz[mb, 1:16], axis=0)
 
     pass_one([(0, dp), (1, dp)])
-    hear_wait(0, "y")
-    hear_send(1, "core")
+    hear_wait(2, "x")
+    hear_send(3, "x")
     wait_rows(cr_sem, 0)
     wait_rows(cr_sem, 1)
     pass_one([(0, mate), (1, mate)])
-    hear_wait(1, "core")
-    hear_send(2, "x")
-    grads_weights(0, y_lo, True)
-    hear_wait(2, "x")
-    hear_send(3, "x")
+    hear_wait(3, "x")
+    hear_send(4, "z")
     wait_rows(gr_sem, 0)
     start_rows(forward, 0)
     pass_one([(0, other)])
-    hear_wait(3, "x")
-    hear_send(4, "z")
+    hear_wait(4, "z")
+    hear_send(5, "z")
     wait_rows(fr_sem, 0)
     pass_one([(0, other_mate)])
     ratio_first(0)
-    hear_wait(4, "z")
-    hear_send(5, "z")
     wait_rows(gr_sem, 1)
     start_rows(forward, 1)
     pass_one([(1, other)])
@@ -253,11 +253,9 @@
     pass_one([(1, other_mate)])
     ratio_first(1)
     ratio_second(0)
+    grads_weights(0, y_lo, True)
+    ratio_second(1)
     grads_weights(1, y_lo, False)
-    ratio_second(1)
-    grads_weights(0, 1 - y_lo, False)
-    grads_weights(1, 1 - y_lo, False)
-    lat_scaled[...] = (lat[...].astype(F32) * sharpness).astype(BF16)
 
     def scale(mb, half):
         r = [
@@ -271,7 +269,7 @@
                 start = mb * BATCH + (2 * half + u) * ROWS
                 at = slice(start, start + ROWS)
                 s = weights[k : k + step, at].astype(F32) * (dots[k : k + step, at] - r[u])
-                weights[k : k + step, at] = s.astype(BF16)
+                scaled[k : k + step, at] = s.astype(BF16)
                 pair = s[:, :128] + s[:, 128:]
                 sums = pair if sums is None else sums + pair
             if mb == 0 and half == 0:
@@ -281,24 +279,20 @@
 
     def latent(mb, half):
         start = mb * BATCH + half * 512
-        product = dot(tab_t[...], weights[:, start : start + 512])
+        product = dot(tab_t[...], scaled[:, start : start + 512])
         for u in range(2):
             lg_part[mb, 2 * half + u] = product[:, u * ROWS : (u + 1) * ROWS].astype(BF16)
-
-    def second_pass(mb):
-        scale(mb, 0)
-        latent(mb, 0)
-        scale(mb, 1)
-        latent(mb, 1)
 
     def grads_scaled(mb, half):
         start = mb * BATCH + half * 512
         at = slice(start, start + 512)
-        grads[...] += dot(weights[:, at], lat_scaled[at, :])
+        grads[...] += dot(scaled[:, at], lat[at, :])
 
     l_core = [
         [
-            remote(lg_part.at[mb, h * 2 + 1 - core], lg_core.at[mb, h], lcs_sem.at[mb], lcr_sem.at[mb], partner)
+            remote(
+                lg_part.at[mb, h * 2 + 1 - core], lg_core.at[mb, h], lcs_sem.at[mb, h], lcr_sem.at[mb, h], partner
+            )
             for h in range(2)
         ]
         for mb in range(2)
@@ -310,14 +304,18 @@
             pl.ds(aligned((no % 2) * 128, 128), 128),
         )
 
-    def chip_peer(i):
-        return device(x + i // 16, y + (i // 4) % 4, z + i, core)
-
-    def l_sum_copy(mb, i):
-        to_y_no = (y + (i // 4) % 4) % 4
-        rows, cols = place_of(((x + i // 16) % 4) * 4 + (z + i) % 4, to_y_no // 2)
-        src = lg_pair.at[mb, to_y_no % 2, rows, cols]
-        return remote(src, lg_sum.at[mb, i], lxs_sem.at[mb], lxr_sem.at[mb], chip_peer(i))
+    own_slot = x * 16 + y * 4 + z
+
+    def l_sum_copy(mb, h, i):
+        to_x, to_hi, to_z = (x + i // 8) % 4, (y_hi + (i // 4) % 2) % 2, (z + i) % 4
+        rows, cols = place_of(to_x * 4 + to_z, to_hi)
+        return remote(
+            lg_pair.at[mb, h, rows, cols],
+            lg_sum.at[mb, own_slot],
+            lxs_sem.at[mb],
+            lxr_sem.at[mb],
+            device(to_x, to_hi * 2 + h, to_z, core),
+        )
 
     def final_place(mb):
         rows, cols = place_of(part_no, y_hi)
@@ -326,26 +324,31 @@
     def l_all_copy(mb, i):
         return remote(lg_final.at[mb], final_place(mb), lgs_sem.at[mb], lgr_sem.at[mb], code_peer(i))
 
-    l_sum = [[l_sum_copy(mb, i) for i in range(1, 64)] for mb in range(2)]
+    l_sum = [[[l_sum_copy(mb, h, i) for i in range(32)] for h in range(2)] for mb in range(2)]
     l_all = [[l_all_copy(mb, i) for i in range(1, 32)] for mb in range(2)]
 
-    def latent_0(mb):
-        for c in l_core[mb]:
+    def latent_0(mb, h):
+        l_core[mb][h].start()
+
+    def latent_1(mb, h):
+        for sem in (lcs_sem, lcr_sem):
+            wait_bytes(lg_core.at[mb, h], sem.at[mb, h])
+        lg_pair[mb, h] = (lg_part[mb, h * 2 + core].astype(F32) + lg_core[mb, h].astype(F32)).astype(BF16)
+        for c in l_sum[mb][h][1:]:
             c.start()
 
-    def latent_1(mb):
-        for sem in (lcs_sem, lcr_sem):
-            wait_bytes(lg_core.at[mb], sem.at[mb])
-        for h in range(2):
-            lg_pair[mb, h] = (lg_part[mb, h * 2 + core].astype(F32) + lg_core[mb, h].astype(F32)).astype(BF16)
-        rows, cols = place_of(part_no, y_hi)
-        lg_sum[mb, 0] = lg_pair[mb, y_lo, rows, cols]
-        for c in l_sum[mb]:
-            c.start()
+        @pl.when(y_lo != h)
+        def _():
+            l_sum[mb][h][0].start()
+
+        @pl.when(y_lo == h)
+        def _():
+            rows, cols = place_of(part_no, y_hi)
+            lg_sum[mb, own_slot] = lg_pair[mb, h, rows, cols]
 
     def latent_2(mb):
         for sem in (lxs_sem, lxr_sem):
-            wait_bytes(lg_sum.at[mb, pl.ds(1, 63)], sem.at[mb])
+            wait_bytes(lg_sum.at[mb, pl.ds(0, 63)], sem.at[mb])
         total = jnp.sum(lg_sum[mb].astype(F32), axis=0).astype(BF16)
         lg_final[mb] = total
         final_place(mb)[...] = total
@@ -360,7 +363,7 @@
     def adam(i, _):
         at = pl.ds(aligned(i * 256, 256), 256)
         t = tab[at, :].astype(F32)
-        sums = jnp.sum(col_sum[at, :], axis=1, keepdims=True) * sharpness
+        sums = jnp.sum(col_sum[at, :], axis=1, keepdims=True)
         grad = grads[at, :] - sums * t
         new_first = first_decay * first_out[at, :] + (1.0 - first_decay) * grad
         new_second = second_decay * second_out[at, :] + (1.0 - second_decay) * grad * grad
@@ -372,25 +375,34 @@
         return 0
 
     ratio_end(0)
-    second_pass(0)
-    latent_0(0)
+    scale(0, 0)
+    latent(0, 0)
+    latent_0(0, 0)
+    scale(0, 1)
+    latent(0, 1)
+    latent_0(0, 1)
+    latent_1(0, 0)
     ratio_end(1)
     scale(1, 0)
-    latent_1(0)
     latent(1, 0)
+    latent_0(1, 0)
+    latent_1(0, 1)
     scale(1, 1)
     latent(1, 1)
-    latent_0(1)
+    latent_0(1, 1)
+    latent_1(1, 0)
     grads_scaled(0, 0)
-    latent_1(1)
+    latent_1(1, 1)
     grads_scaled(0, 1)
     grads_scaled(1, 0)
+    latent_2(0)
     grads_scaled(1, 1)
+    latent_2(1)
+    grads_weights(0, 1 - y_lo, False)
+    grads_weights(1, 1 - y_lo, False)
     mom1_copy.wait()
     mom2_copy.wait()
-    latent_2(0)
     lax.fori_loop(0, 8, adam, 0)
-    latent_2(1)
     latent_3(0)
     latent_3(1)
     for sems in (cs_sem, gs_sem, fs_sem):
@@ -424,11 +436,11 @@
         scratch_shapes=[
             pltpu.VMEM((ALL, WIDTH), BF16),
             pltpu.VMEM((ALL, WIDTH), BF16),
-            pltpu.VMEM((ALL, WIDTH), BF16),
             pltpu.VMEM((4, 2, ROWS), F32),
             pltpu.VMEM((CODES, WIDTH), BF16),
             pltpu.VMEM((WIDTH, CODES), BF16),
             pltpu.VMEM((CODES, 128), F32),
+            pltpu.VMEM((CODES, ALL), BF16),
             pltpu.VMEM((CODES, ALL), BF16),
             pltpu.VMEM((CODES, ALL), F32),
             pltpu.VMEM((CODES, WIDTH), F32),
@@ -448,10 +460,10 @@
             dma((8,)),
             dma((3,)), dma((3,)), dma((3,)), dma((3,)), dma((3,)), dma((3,)),
             dma((2,)), dma((2,)), dma((2,)), dma((2,)),
-            dma((2,)), dma((2,)), dma((2,)), dma((2,)), dma((2,)), dma((2,)),
+            dma((2, 2)), dma((2, 2)), dma((2,)), dma((2,)), dma((2,)), dma((2,)),
         ],
         compiler_params=pltpu.CompilerParams(
-            collective_id=0, has_side_effects=True, vmem_limit_bytes=40 * 1024 * 1024
+            collective_id=0, has_side_effects=True, vmem_limit_bytes=47 * 1024 * 1024
         ),
     )(*[pltpu.with_memory_space_constraint(a, pltpu.HBM) for a in arrays])
     code_array = jax.ShapeDtypeStruct(code_shape, F32)

time: 51.2 us -> 47.1 us (0.920); the launches traced: 51.1 us -> 46.3 us
  Pallas kernels: 50.3 us -> 45.5 us
    pallas_call x1, Pallas kernels: 46.9 us -> 42 us  [body(): pl.pallas_call(kernel, name='soft_codebook', out_shape=(pltpu.VMEM((2, WI...]
where the time goes in v4:
time: 47.1 us; the launch traced here: 46.3 us
  Pallas kernels  45.5 us (97%)
  between operations  0.8 us (2%)
    pallas_call x1, Pallas kernels, body(): pl.pallas_call(kernel, name='soft_codebook', out_shape=(pltpu.VMEM((2, WI...  42 us
    pallas_call x1, Pallas kernels, body(): pl.pallas_call(write_out, name='write_out', out_shape=(jax.ShapeDtypeStru...  3.45 us

profile of v4, /device:TPU:0, one launch (start us, length us, event | category | flops | bytes accessed | tf_op | source)
XLA Modules:
  0.0 46.3 jit_solution(8185007876128551831)
XLA Ops:
  0.6 42.0 %soft_codebook.1 = (bf16[2,256,256]{2,1,0:T(8,128)(2,1)S(1)}, f32[2048,256]{1,0:T(8,128)S(1)}, f32[2048,256]{1,0:T(8,128)S(1)}, f32[2048,256]{1,0:T(8,128)S(1)}) custom-call(bf16[2,256,256]{2,1,0:T(8,128)(2,1)} %lat_in.1, bf16[2,256,256]{2,1,0:T(8,128)(2,1)} %cot_in.1, f32[2,256]{1,0:T(2,128)} %lse_in.1, f32[2048,256]{1,0:T(8,128)} %code_in.1, ...), custom_call_target="tpu_custom_call" | custom-call | tf_op jit(solution)/shard_map/soft_codebook/pallas_call | solution.py:430
  42.7 3.5 %write_out.1 = (bf16[2,256,256]{2,1,0:T(8,128)(2,1)}, f32[2048,256]{1,0:T(8,128)}, f32[2048,256]{1,0:T(8,128)}, f32[2048,256]{1,0:T(8,128)}) custom-call(bf16[2,256,256]{2,1,0:T(8,128)(2,1)S(1)} %get-tuple-element.8.lg_in, f32[2048,256]{1,0:T(8,128)S(1)} %get-tuple-element.9.code_in, f32[2048,256]{1,0:T(8,128)S(1)} %get-tuple-element.10.first_in, ...), custom_call_target="tpu_custom_call" | custom-call | tf_op jit(solution)/shard_map/write_out/pallas_call | solution.py:470

commit v5 on v4

--- a/solution.py
+++ b/solution.py
@@ -35,19 +35,12 @@
     return ((y % 2) * 2 + core, x * 8 + (y // 2) * 4 + z)
 
 
-def dot_nt(a, b):
-    return lax.dot_general(a, b, (((1,), (1,)), ((), ())), preferred_element_type=F32)
-
-
-def dot(a, b):
-    return jnp.dot(a, b, preferred_element_type=F32)
-
-
 def aligned(v, n):
     return pl.multiple_of(v, n)
 
 
 def kernel(
+    acc_grads, acc_work,
     lat_in, cot_in, lse_in, code_in, first_in, second_in,
     lg_out, code_out, first_out, second_out,
     lat, cot, lse, tab, tab_t, bias, weights, scaled, dots, grads, col_sum,
@@ -145,8 +138,6 @@
     start_rows(to_partner, 1)
 
     book_copy.wait()
-    hear_wait(0, "y")
-    hear_send(1, "core")
 
     def make_table(i, _):
         at = pl.ds(aligned(i * 256, 256), 256)
@@ -162,37 +153,65 @@
     start_rows(to_y, 1)
     mom1_copy.start()
     mom2_copy.start()
-    hear_wait(1, "core")
-    hear_send(2, "x")
+    hear_wait(0, "y")
+    hear_send(1, "core")
+
+    staged = [0, 0]
+
+    def push(rhs, unit, transpose=False):
+        staged[unit] = 1 - staged[unit]
+        pltpu.matmul_push_rhs(rhs, staged[unit], unit, transpose=transpose)
+        return staged[unit]
 
     def pass_one(pairs):
         places = [rows_of(mb, owner) for mb, owner in pairs]
         shifts = [lse[owner, mb : mb + 1, :] * LOG2E for mb, owner in pairs]
         totals = [jnp.zeros((8, ROWS), F32) for _ in pairs]
         step = 256
-        for k in range(0, CODES, step):
-            t = tab[k : k + step, :]
+        tiles = [(i, k) for i in range(len(pairs)) for k in range(0, CODES, step)]
+
+        def multiply(n):
+            i, k = tiles[n]
+            for unit, rows in enumerate((lat, cot)):
+                load = push(rows[places[i], :], unit, transpose=True) if k == 0 else None
+                pltpu.matmul_acc_lhs(acc_work[unit][n % 2], tab[k : k + step, :], load)
+
+        multiply(0)
+        for n, (i, k) in enumerate(tiles):
+            if n + 1 < len(tiles):
+                multiply(n + 1)
             b = bias[k : k + step, :]
-            b = jnp.concatenate([b, b], axis=1)
-            for i, at in enumerate(places):
-                logits = dot_nt(t, lat[at, :])
-                inner = dot_nt(t, cot[at, :]) * sharpness
-                w = jnp.exp2(logits * (sharpness * LOG2E) - b - shifts[i])
-                totals[i] = totals[i] + jnp.sum((w * inner).reshape(step // 8, 8, ROWS), axis=0)
-                weights[k : k + step, at] = w.astype(BF16)
-                dots[k : k + step, at] = inner
+            logits = pltpu.matmul_pop(acc_work[0][n % 2])
+            inner = pltpu.matmul_pop(acc_work[1][n % 2]) * sharpness
+            w = jnp.exp2(logits * (sharpness * LOG2E) - jnp.concatenate([b, b], axis=1) - shifts[i])
+            totals[i] = totals[i] + jnp.sum((w * inner).reshape(step // 8, 8, ROWS), axis=0)
+            weights[k : k + step, places[i]] = w.astype(BF16)
+            dots[k : k + step, places[i]] = inner
         for (mb, owner), total in zip(pairs, totals):
             row = jnp.sum(total, axis=0, keepdims=True)
             part[mb, pl.ds(owner * 2, 1), :] = row[:, :128]
             part[mb, pl.ds(owner * 2 + 1, 1), :] = row[:, 128:]
 
-    def grads_weights(mb, half, first):
-        at = pl.ds(aligned(mb * BATCH + half * 512, 512), 512)
-        product = dot(weights[:, at], cot[at, :])
-        if first:
-            grads[...] = product
-        else:
-            grads[...] += product
+    def add_grads(terms, half, first=False):
+        codes = [slice(half * 1024 + unit * 512, half * 1024 + unit * 512 + 512) for unit in range(2)]
+        for left, right, start in terms:
+            at = pl.ds(start, ROWS)
+            for unit in range(2):
+                load = push(right[at, :], unit)
+                pltpu.matmul_acc_lhs(acc_grads[unit], left[codes[unit], at], load)
+        for unit in range(2):
+            total = pltpu.matmul_pop(acc_grads[unit])
+            if first:
+                grads[codes[unit], :] = total
+            else:
+                grads[codes[unit], :] += total
+
+    def grads_weights(chip, half, first=False):
+        starts = [aligned(mb * BATCH + chip * 512 + c * ROWS, ROWS) for mb in range(2) for c in range(2)]
+        add_grads([(weights, cot, start) for start in starts], half, first)
+
+    def grads_scaled(mb, half):
+        add_grads([(scaled, lat, mb * BATCH + c * ROWS) for c in range(4)], half)
 
     other = (1 - y_lo) * 2 + core
     forward = row_copies(other, fs_sem, fr_sem, partner, partner)
@@ -230,63 +249,62 @@
         ratio[mb] = part_s[mb] + jnp.sum(part_xz[mb, 1:16], axis=0)
 
     pass_one([(0, dp), (1, dp)])
-    hear_wait(2, "x")
-    hear_send(3, "x")
+    hear_wait(1, "core")
+    hear_send(2, "x")
     wait_rows(cr_sem, 0)
     wait_rows(cr_sem, 1)
     pass_one([(0, mate), (1, mate)])
-    hear_wait(3, "x")
-    hear_send(4, "z")
+    hear_wait(2, "x")
+    hear_send(3, "x")
     wait_rows(gr_sem, 0)
     start_rows(forward, 0)
     pass_one([(0, other)])
-    hear_wait(4, "z")
-    hear_send(5, "z")
+    hear_wait(3, "x")
+    hear_send(4, "z")
     wait_rows(fr_sem, 0)
     pass_one([(0, other_mate)])
     ratio_first(0)
+    hear_wait(4, "z")
+    hear_send(5, "z")
     wait_rows(gr_sem, 1)
     start_rows(forward, 1)
     pass_one([(1, other)])
-    hear_wait(5, "z")
     wait_rows(fr_sem, 1)
     pass_one([(1, other_mate)])
     ratio_first(1)
+    hear_wait(5, "z")
     ratio_second(0)
-    grads_weights(0, y_lo, True)
+    grads_weights(y_lo, 0, True)
+    grads_weights(y_lo, 1, True)
     ratio_second(1)
-    grads_weights(1, y_lo, False)
-
-    def scale(mb, half):
+    grads_weights(1 - y_lo, 0)
+    grads_weights(1 - y_lo, 1)
+
+    def second_pass(mb, half):
         r = [
             jnp.concatenate([ratio[mb, 2 * u : 2 * u + 1, :], ratio[mb, 2 * u + 1 : 2 * u + 2, :]], axis=1)
             for u in (2 * half, 2 * half + 1)
         ]
         step = 256
         for k in range(0, CODES, step):
-            sums = None
+            left = tab_t[:, k : k + step]
+            total = None
             for u in range(2):
                 start = mb * BATCH + (2 * half + u) * ROWS
                 at = slice(start, start + ROWS)
                 s = weights[k : k + step, at].astype(F32) * (dots[k : k + step, at] - r[u])
-                scaled[k : k + step, at] = s.astype(BF16)
+                s_half = s.astype(BF16)
+                scaled[k : k + step, at] = s_half
                 pair = s[:, :128] + s[:, 128:]
-                sums = pair if sums is None else sums + pair
+                total = pair if total is None else total + pair
+                load = push(s_half, u)
+                pltpu.matmul_acc_lhs(acc_work[u][0], left, load)
             if mb == 0 and half == 0:
-                col_sum[k : k + step, :] = sums
+                col_sum[k : k + step, :] = total
             else:
-                col_sum[k : k + step, :] += sums
-
-    def latent(mb, half):
-        start = mb * BATCH + half * 512
-        product = dot(tab_t[...], scaled[:, start : start + 512])
+                col_sum[k : k + step, :] += total
         for u in range(2):
-            lg_part[mb, 2 * half + u] = product[:, u * ROWS : (u + 1) * ROWS].astype(BF16)
-
-    def grads_scaled(mb, half):
-        start = mb * BATCH + half * 512
-        at = slice(start, start + 512)
-        grads[...] += dot(scaled[:, at], lat[at, :])
+            lg_part[mb, 2 * half + u] = pltpu.matmul_pop(acc_work[u][0]).astype(BF16)
 
     l_core = [
         [
@@ -314,7 +332,7 @@
             lg_sum.at[mb, own_slot],
             lxs_sem.at[mb],
             lxr_sem.at[mb],
-            device(to_x, to_hi * 2 + h, to_z, core),
+            device(to_x, to_hi * 2 + 1 - h, to_z, core),
         )
 
     def final_place(mb):
@@ -322,10 +340,11 @@
         return lg_all.at[mb, rows, cols]
 
     def l_all_copy(mb, i):
-        return remote(lg_final.at[mb], final_place(mb), lgs_sem.at[mb], lgr_sem.at[mb], code_peer(i))
+        to = device(x + i // 8, ((y_hi + i // 4) % 2) * 2 + 1 - y_lo, z + i, core)
+        return remote(lg_final.at[mb], final_place(mb), lgs_sem.at[mb], lgr_sem.at[mb], to)
 
     l_sum = [[[l_sum_copy(mb, h, i) for i in range(32)] for h in range(2)] for mb in range(2)]
-    l_all = [[l_all_copy(mb, i) for i in range(1, 32)] for mb in range(2)]
+    l_all = [[l_all_copy(mb, i) for i in range(32)] for mb in range(2)]
 
     def latent_0(mb, h):
         l_core[mb][h].start()
@@ -337,11 +356,11 @@
         for c in l_sum[mb][h][1:]:
             c.start()
 
-        @pl.when(y_lo != h)
+        @pl.when(y_lo == h)
         def _():
             l_sum[mb][h][0].start()
 
-        @pl.when(y_lo == h)
+        @pl.when(y_lo != h)
         def _():
             rows, cols = place_of(part_no, y_hi)
             lg_sum[mb, own_slot] = lg_pair[mb, h, rows, cols]
@@ -351,14 +370,13 @@
             wait_bytes(lg_sum.at[mb, pl.ds(0, 63)], sem.at[mb])
         total = jnp.sum(lg_sum[mb].astype(F32), axis=0).astype(BF16)
         lg_final[mb] = total
-        final_place(mb)[...] = total
         for c in l_all[mb]:
             c.start()
 
     def latent_3(mb):
         for sem in (lgs_sem, lgr_sem):
-            wait_bytes(lg_sum.at[mb, pl.ds(1, 31)], sem.at[mb])
-        lg_out[mb] = lg_all[mb]
+            wait_bytes(lg_sum.at[mb, pl.ds(0, 32)], sem.at[mb])
+        lg_out[mb] = lg_all[mb].T
 
     def adam(i, _):
         at = pl.ds(aligned(i * 256, 256), 256)
@@ -375,34 +393,29 @@
         return 0
 
     ratio_end(0)
-    scale(0, 0)
-    latent(0, 0)
+    second_pass(0, 0)
     latent_0(0, 0)
-    scale(0, 1)
-    latent(0, 1)
+    second_pass(0, 1)
     latent_0(0, 1)
     latent_1(0, 0)
     ratio_end(1)
-    scale(1, 0)
-    latent(1, 0)
+    second_pass(1, 0)
     latent_0(1, 0)
     latent_1(0, 1)
-    scale(1, 1)
-    latent(1, 1)
+    second_pass(1, 1)
     latent_0(1, 1)
     latent_1(1, 0)
     grads_scaled(0, 0)
     latent_1(1, 1)
     grads_scaled(0, 1)
     grads_scaled(1, 0)
-    latent_2(0)
     grads_scaled(1, 1)
-    latent_2(1)
-    grads_weights(0, 1 - y_lo, False)
-    grads_weights(1, 1 - y_lo, False)
     mom1_copy.wait()
     mom2_copy.wait()
-    lax.fori_loop(0, 8, adam, 0)
+    lax.fori_loop(0, 3, adam, 0)
+    latent_2(0)
+    latent_2(1)
+    lax.fori_loop(3, 8, adam, 0)
     latent_3(0)
     latent_3(1)
     for sems in (cs_sem, gs_sem, fs_sem):
@@ -410,15 +423,18 @@
         wait_rows(sems, 1)
 
 
-def write_out(lg_in, code_in, first_in, second_in, lg_out, code_out, first_out, second_out, sems):
-    copies = [
-        pltpu.make_async_copy(src, dst, sems.at[i])
-        for i, (src, dst) in enumerate([(code_in, code_out), (first_in, first_out), (second_in, second_out)])
-    ]
+def with_sums(*refs):
+    def run(g0, g1, w00, w01, w10, w11):
+        kernel((g0, g1), ((w00, w01), (w10, w11)), *refs)
+
+    sums = lambda unit, rows: pltpu.ACC(unit)((rows, WIDTH), F32)
+    pl.run_scoped(run, sums(0, 512), sums(1, 512), *[sums(unit, 256) for unit in (0, 0, 1, 1)])
+
+
+def write_out(*refs):
+    copies = [pltpu.make_async_copy(refs[i], refs[i + 4], refs[8].at[i]) for i in range(4)]
     for c in copies:
         c.start()
-    for mb in range(2):
-        lg_out[mb] = lg_in[mb].T
     for c in copies:
         c.wait()
 
@@ -428,9 +444,9 @@
     any_spec, vmem_spec = pl.BlockSpec(memory_space=pl.ANY), pl.BlockSpec(memory_space=pltpu.VMEM)
     code_shape, rows_shape = (CODES, WIDTH), (2, ROWS, WIDTH)
     parts = pl.pallas_call(
-        kernel,
+        with_sums,
         name="soft_codebook",
-        out_shape=(pltpu.VMEM((2, WIDTH, ROWS), BF16),) + (pltpu.VMEM(code_shape, F32),) * 3,
+        out_shape=(pltpu.VMEM(rows_shape, BF16),) + (pltpu.VMEM(code_shape, F32),) * 3,
         in_specs=[pl.BlockSpec(memory_space=pltpu.HBM)] * 6,
         out_specs=[vmem_spec] * 4,
         scratch_shapes=[
@@ -472,16 +488,20 @@
         name="write_out",
         out_shape=(jax.ShapeDtypeStruct(rows_shape, BF16), code_array, code_array, code_array),
         in_specs=[vmem_spec] * 4,
-        out_specs=[vmem_spec] + [any_spec] * 3,
-        scratch_shapes=[dma((3,))],
+        out_specs=[any_spec] * 4,
+        scratch_shapes=[dma((4,))],
         compiler_params=pltpu.CompilerParams(vmem_limit_bytes=8 * 1024 * 1024),
     )(*[pltpu.with_memory_space_constraint(p, pltpu.VMEM) for p in parts])
 
 
 def solution(mesh):
     rows, codes = P(None, "dp", None), P(("dp", "code"), None)
+    def run(*arrays):
+        with jax.sharding.use_abstract_mesh(mesh.abstract_mesh):
+            return body(*arrays)
+
     return jax.shard_map(
-        body,
+        run,
         mesh=mesh,
         in_specs=(rows, rows, P(None, "dp"), codes, codes, codes),
         out_specs=(rows, codes, codes, codes),

time: 47.1 us -> 45.3 us (0.962); the launches traced: 46.3 us -> 45.2 us
  Pallas kernels: 45.5 us -> 44.4 us
    pallas_call x1, Pallas kernels: 3.45 us -> 2.82 us  [body(): pl.pallas_call(write_out, name='write_out', out_shape=(jax.ShapeDtypeStru...]
where the time goes in v5:
time: 45.3 us; the launch traced here: 45.2 us
  Pallas kernels  44.4 us (98%)
  between operations  0.8 us (2%)
    pallas_call x1, Pallas kernels, body(): pl.pallas_call(with_sums, name='soft_codebook', out_shape=(pltpu.VMEM(row...  41.6 us
    pallas_call x1, Pallas kernels, body(): pl.pallas_call(write_out, name='write_out', out_shape=(jax.ShapeDtypeStru...  2.82 us

profile of v5, /device:TPU:0, one launch (start us, length us, event | category | flops | bytes accessed | tf_op | source)
XLA Modules:
  0.0 45.2 jit_solution(12199572120013835366)
XLA Ops:
  0.6 41.6 %soft_codebook.1 = (bf16[2,256,256]{2,1,0:T(8,128)(2,1)S(1)}, f32[2048,256]{1,0:T(8,128)S(1)}, f32[2048,256]{1,0:T(8,128)S(1)}, f32[2048,256]{1,0:T(8,128)S(1)}) custom-call(bf16[2,256,256]{2,1,0:T(8,128)(2,1)} %refs_0_.1, bf16[2,256,256]{2,1,0:T(8,128)(2,1)} %refs_1_.1, f32[2,256]{1,0:T(2,128)} %refs_2_.1, f32[2048,256]{1,0:T(8,128)} %refs_3_.1, ...), custom_call_target="tpu_custom_call" | custom-call | tf_op jit(solution)/shard_map/soft_codebook/pallas_call | solution.py:446
  42.2 2.8 %write_out.1 = (bf16[2,256,256]{2,1,0:T(8,128)(2,1)}, f32[2048,256]{1,0:T(8,128)}, f32[2048,256]{1,0:T(8,128)}, f32[2048,256]{1,0:T(8,128)}) custom-call(bf16[2,256,256]{2,1,0:T(8,128)(2,1)S(1)} %get-tuple-element.8.refs_0_, f32[2048,256]{1,0:T(8,128)S(1)} %get-tuple-element.9.refs_1_, f32[2048,256]{1,0:T(8,128)S(1)} %get-tuple-element.10.refs_2_, ...), custom_call_target="tpu_custom_call" | custom-call | tf_op jit(solution)/shard_map/write_out/pallas_call | solution.py:486

commit v6 on v5

--- a/solution.py
+++ b/solution.py
@@ -33,6 +33,14 @@
 def device(x, y, z, core):
     x, y, z, core = x % 4, y % 4, z % 4, core % 2
     return ((y % 2) * 2 + core, x * 8 + (y // 2) * 4 + z)
+
+
+def away(n):
+    return min(n % 4, 4 - n % 4)
+
+
+def far_first(peers, distance):
+    return sorted(peers, key=distance, reverse=True)
 
 
 def aligned(v, n):
@@ -221,13 +229,13 @@
     def ratio_y(mb):
         return [
             remote(part.at[mb], part_y.at[mb, i], ays_sem.at[mb], ayr_sem.at[mb], yc_peer(i))
-            for i in range(1, 8)
+            for i in far_first(range(1, 8), lambda i: away(i // 2) + i % 2)
         ]
 
     def ratio_xz(mb):
         return [
             remote(part_s.at[mb], part_xz.at[mb, i], axs_sem.at[mb], axr_sem.at[mb], xz_peer(i))
-            for i in range(1, 16)
+            for i in far_first(range(1, 16), lambda i: away(i // 4) + away(i))
         ]
 
     ry, rx = [ratio_y(0), ratio_y(1)], [ratio_xz(0), ratio_xz(1)]
@@ -344,7 +352,9 @@
         return remote(lg_final.at[mb], final_place(mb), lgs_sem.at[mb], lgr_sem.at[mb], to)
 
     l_sum = [[[l_sum_copy(mb, h, i) for i in range(32)] for h in range(2)] for mb in range(2)]
-    l_all = [[l_all_copy(mb, i) for i in range(32)] for mb in range(2)]
+    l_all = [
+        [l_all_copy(mb, i) for i in far_first(range(32), lambda i: away(i // 8) + away(i))] for mb in range(2)
+    ]
 
     def latent_0(mb, h):
         l_core[mb][h].start()
@@ -353,8 +363,8 @@
         for sem in (lcs_sem, lcr_sem):
             wait_bytes(lg_core.at[mb, h], sem.at[mb, h])
         lg_pair[mb, h] = (lg_part[mb, h * 2 + core].astype(F32) + lg_core[mb, h].astype(F32)).astype(BF16)
-        for c in l_sum[mb][h][1:]:
-            c.start()
+        for i in far_first(range(1, 32), lambda i: away(i // 8) + away(i) + (i // 4) % 2):
+            l_sum[mb][h][i].start()
 
         @pl.when(y_lo == h)
         def _():

time: 45.3 us -> 44 us (0.971)
  Pallas kernels: 44.4 us -> 42.9 us
    pallas_call x1, Pallas kernels: 41.6 us -> 40.1 us  [body(): pl.pallas_call(with_sums, name='soft_codebook', out_shape=(pltpu.VMEM(row...]
where the time goes in v6:
time: 44 us; the launch traced here: 43.7 us
  Pallas kernels  42.9 us (98%)
  between operations  0.8 us (2%)
    pallas_call x1, Pallas kernels, body(): pl.pallas_call(with_sums, name='soft_codebook', out_shape=(pltpu.VMEM(row...  40.1 us
    pallas_call x1, Pallas kernels, body(): pl.pallas_call(write_out, name='write_out', out_shape=(jax.ShapeDtypeStru...  2.82 us

profile of v6, /device:TPU:0, one launch (start us, length us, event | category | flops | bytes accessed | tf_op | source)
XLA Modules:
  0.0 43.7 jit_solution(3165721730037694369)
XLA Ops:
  0.6 40.1 %soft_codebook.1 = (bf16[2,256,256]{2,1,0:T(8,128)(2,1)S(1)}, f32[2048,256]{1,0:T(8,128)S(1)}, f32[2048,256]{1,0:T(8,128)S(1)}, f32[2048,256]{1,0:T(8,128)S(1)}) custom-call(bf16[2,256,256]{2,1,0:T(8,128)(2,1)} %refs_0_.1, bf16[2,256,256]{2,1,0:T(8,128)(2,1)} %refs_1_.1, f32[2,256]{1,0:T(2,128)} %refs_2_.1, f32[2048,256]{1,0:T(8,128)} %refs_3_.1, ...), custom_call_target="tpu_custom_call" | custom-call | tf_op jit(solution)/shard_map/soft_codebook/pallas_call | solution.py:456
  40.7 2.8 %write_out.1 = (bf16[2,256,256]{2,1,0:T(8,128)(2,1)}, f32[2048,256]{1,0:T(8,128)}, f32[2048,256]{1,0:T(8,128)}, f32[2048,256]{1,0:T(8,128)}) custom-call(bf16[2,256,256]{2,1,0:T(8,128)(2,1)S(1)} %get-tuple-element.8.refs_0_, f32[2048,256]{1,0:T(8,128)S(1)} %get-tuple-element.9.refs_1_, f32[2048,256]{1,0:T(8,128)S(1)} %get-tuple-element.10.refs_2_, ...), custom_call_target="tpu_custom_call" | custom-call | tf_op jit(solution)/shard_map/write_out/pallas_call | solution.py:496

commit v7 on v6

--- a/solution.py
+++ b/solution.py
@@ -143,7 +143,6 @@
     start_rows(to_y, 0)
     hear_send(0, "y")
     start_rows(to_partner, 0)
-    start_rows(to_partner, 1)
 
     book_copy.wait()
 
@@ -158,6 +157,7 @@
         return 0
 
     lax.fori_loop(0, CODES // 256, make_table, 0)
+    start_rows(to_partner, 1)
     start_rows(to_y, 1)
     mom1_copy.start()
     mom2_copy.start()
@@ -220,6 +220,15 @@
 
     def grads_scaled(mb, half):
         add_grads([(scaled, lat, mb * BATCH + c * ROWS) for c in range(4)], half)
+        for k in range(half * 1024, half * 1024 + 1024, 128):
+            total = None
+            for c in range(mb * BATCH, (mb + 1) * BATCH, 128):
+                block = scaled[k : k + 128, c : c + 128].astype(F32)
+                total = block if total is None else total + block
+            if mb == 0:
+                col_sum[k : k + 128, :] = total
+            else:
+                col_sum[k : k + 128, :] += total
 
     other = (1 - y_lo) * 2 + core
     forward = row_copies(other, fs_sem, fr_sem, partner, partner)
@@ -296,21 +305,14 @@
         step = 256
         for k in range(0, CODES, step):
             left = tab_t[:, k : k + step]
-            total = None
             for u in range(2):
                 start = mb * BATCH + (2 * half + u) * ROWS
                 at = slice(start, start + ROWS)
                 s = weights[k : k + step, at].astype(F32) * (dots[k : k + step, at] - r[u])
                 s_half = s.astype(BF16)
                 scaled[k : k + step, at] = s_half
-                pair = s[:, :128] + s[:, 128:]
-                total = pair if total is None else total + pair
                 load = push(s_half, u)
                 pltpu.matmul_acc_lhs(acc_work[u][0], left, load)
-            if mb == 0 and half == 0:
-                col_sum[k : k + step, :] = total
-            else:
-                col_sum[k : k + step, :] += total
         for u in range(2):
             lg_part[mb, 2 * half + u] = pltpu.matmul_pop(acc_work[u][0]).astype(BF16)
 

time: 44 us -> 43.7 us (level)
  no operation moved by 1% of the time
where the time goes in v7:
time: 43.7 us; the launch traced here: 43.6 us
  Pallas kernels  42.8 us (98%)
  between operations  0.8 us (2%)
    pallas_call x1, Pallas kernels, body(): pl.pallas_call(with_sums, name='soft_codebook', out_shape=(pltpu.VMEM(row...  39.9 us
    pallas_call x1, Pallas kernels, body(): pl.pallas_call(write_out, name='write_out', out_shape=(jax.ShapeDtypeStru...  2.82 us

profile of v7, /device:TPU:0, one launch (start us, length us, event | category | flops | bytes accessed | tf_op | source)
XLA Modules:
  0.0 43.6 jit_solution(13631914126983126065)
XLA Ops:
  0.6 39.9 %soft_codebook.1 = (bf16[2,256,256]{2,1,0:T(8,128)(2,1)S(1)}, f32[2048,256]{1,0:T(8,128)S(1)}, f32[2048,256]{1,0:T(8,128)S(1)}, f32[2048,256]{1,0:T(8,128)S(1)}) custom-call(bf16[2,256,256]{2,1,0:T(8,128)(2,1)} %refs_0_.1, bf16[2,256,256]{2,1,0:T(8,128)(2,1)} %refs_1_.1, f32[2,256]{1,0:T(2,128)} %refs_2_.1, f32[2048,256]{1,0:T(8,128)} %refs_3_.1, ...), custom_call_target="tpu_custom_call" | custom-call | tf_op jit(solution)/shard_map/soft_codebook/pallas_call | solution.py:458
  40.6 2.8 %write_out.1 = (bf16[2,256,256]{2,1,0:T(8,128)(2,1)}, f32[2048,256]{1,0:T(8,128)}, f32[2048,256]{1,0:T(8,128)}, f32[2048,256]{1,0:T(8,128)}) custom-call(bf16[2,256,256]{2,1,0:T(8,128)(2,1)S(1)} %get-tuple-element.8.refs_0_, f32[2048,256]{1,0:T(8,128)S(1)} %get-tuple-element.9.refs_1_, f32[2048,256]{1,0:T(8,128)S(1)} %get-tuple-element.10.refs_2_, ...), custom_call_target="tpu_custom_call" | custom-call | tf_op jit(solution)/shard_map/write_out/pallas_call | solution.py:498
